TPU v7x, 32 devices: a whole 2x2x4 slice. The times are simulated.
32 devices in a mesh: blk: 32 (over z, y, x, core).
Axes of the slice: x: 2, y: 2, z: 4, core: 2. Of those that a mesh axis runs over, the one named last changes fastest.
Arguments:
- images: bfloat16 [12800, 768], P('blk'), may hold values from -6 to 6
- captions: bfloat16 [20480, 768], P('blk'), may hold values from -6 to 6
- img_gain1: bfloat16 [768], replicated, may hold values from 0.5 to 1.5
- img_bias1: bfloat16 [768], replicated, may hold values from -3 to 3
- img_qkv: bfloat16 [1769472], P('blk'), may hold values from -0.21875 to 0.21875
- img_out: bfloat16 [589824], P('blk'), may hold values from -0.5 to 0.5
- img_gain2: bfloat16 [768], replicated, may hold values from 0.5 to 1.5
- img_bias2: bfloat16 [768], replicated, may hold values from -3 to 3
- img_up: bfloat16 [2359296], P('blk'), may hold values from -0.21875 to 0.21875
- img_down: bfloat16 [2359296], P('blk'), may hold values from -0.109375 to 0.109375
- txt_gain1: float32 [768], replicated, may hold values from 0.5 to 1.5
- txt_bias1: float32 [768], replicated, may hold values from -3 to 3
- txt_qkv: bfloat16 [768, 2304], replicated, may hold values from -0.21875 to 0.21875
- txt_out: bfloat16 [768, 768], replicated, may hold values from -0.4375 to 0.4375
- txt_gain2: float32 [768], replicated, may hold values from 0.5 to 1.5
- txt_bias2: float32 [768], replicated, may hold values from -3 to 3
- txt_up: bfloat16 [768, 3072], replicated, may hold values from -0.21875 to 0.21875
- txt_down: bfloat16 [3072, 768], replicated, may hold values from -0.109375 to 0.109375
- counts: int32 [256], P('blk'), may hold values from 1 to 5, as said below
- matches: int32 [1280, 256], P('blk'), may hold values 0 or 1
Outputs:
- loss: float32 [], replicated
- caption_grad: float32 [20480, 768], P('blk')
- grad_gain1: float32 [768], replicated
- grad_bias1: float32 [768], replicated
- grad_qkv: float32 [1769472], P('blk')
- grad_out: float32 [589824], P('blk')
- grad_gain2: float32 [768], replicated
- grad_bias2: float32 [768], replicated
- grad_up: float32 [2359296], P('blk')
- grad_down: float32 [2359296], P('blk')
Inputs may be any that keep to these rules, and one draw needn't show every extreme that they name: `counts`: each image has 1 to 5 captions; in every draw all 8 images of one block have 5, so that block's 40 caption slots are all live.
All inputs are finite; a program needn't handle non-finite values. No bound on the sum of `matches` on one device may be relied on, other than what follows from the above.
Results may differ from a plain program's by a relative error of at most 0.015.
Values may be sent and summed in bfloat16 or wider, within the bound.
No kernel may reach another device: no remote copies, remote signals or barrier semaphores. Data moves between devices by JAX's collectives and lax.ppermute only.
A program may use at most 192 MiB of HBM per device.

v0:
```python
import functools

import jax
import jax.numpy as jnp
from jax import lax
from jax.experimental import pallas as pl
from jax.experimental.pallas import tpu as pltpu
from jax.sharding import PartitionSpec as P

D = 768
FF = 3072
HEAD = 64
HEADS = D // HEAD
IMG_LEN = 50
TXT_LEN = 16
AXIS = "blk"

norm_eps = 1e-06
logit_scale = 50.0
f32 = jnp.float32
bf16 = jnp.bfloat16


def swapped(value, mask):
    peers = lax.axis_size(AXIS)
    return lax.ppermute(value, AXIS, [(i, i ^ mask) for i in range(peers)])


def bit_masks():
    peers = lax.axis_size(AXIS)
    return [1 << k for k in range(peers.bit_length() - 1)]


def gathered(block):
    own = lax.axis_index(AXIS)
    held = block[None]
    for mask in reversed(bit_masks()):
        other = swapped(held, mask)
        upper = (own & mask) > 0
        first = jnp.where(upper, other, held)
        second = jnp.where(upper, held, other)
        held = jnp.stack([first, second], axis=1).reshape((-1,) + block.shape)
    return held


def spread(block):
    peers = lax.axis_size(AXIS)
    copies = jnp.broadcast_to(block[None], (peers,) + block.shape)
    return lax.all_to_all(copies, AXIS, split_axis=0, concat_axis=0, tiled=True)


def stage_orders():
    masks = bit_masks()
    head, tail = masks[:-2], masks[-2:]
    order_a = list(head)
    order_b = list(head)
    for k in range(1, len(head) - 1, 2):
        order_b[k], order_b[k + 1] = order_b[k + 1], order_b[k]
    return order_a, order_b, tail


def row_order(order, tail):
    peers = lax.axis_size(AXIS)
    own = lax.axis_index(AXIS)
    per = D // peers
    bits = list(order) + list(reversed(tail))
    places = lax.iota(jnp.int32, D)
    block = places // per
    target = jnp.zeros_like(block) + own
    for k, mask in enumerate(bits):
        target = target ^ (((block >> (len(bits) - 1 - k)) & 1) * mask)
    source = target * per + places % per
    return (source[:, None] == lax.iota(jnp.int32, D)[None, :]).astype(bf16)


def placed(order, values):
    return mul_bt(order, values).astype(bf16)


def summed_pair(kept, got):
    return (kept.astype(f32) + got.astype(f32)).astype(bf16)


def scattered(keep_a, send_a, keep_b, send_b):
    order_a, order_b, tail = stage_orders()
    for k, (mask_a, mask_b) in enumerate(zip(order_a, order_b)):
        got_a = swapped(send_a, mask_a)
        got_b = swapped(send_b, mask_b)
        half = keep_a.shape[0] // 2
        if k + 1 < len(order_a):
            send_a = summed_pair(keep_a[half:], got_a[half:])
            send_b = summed_pair(keep_b[half:], got_b[half:])
            keep_a = summed_pair(keep_a[:half], got_a[:half])
            keep_b = summed_pair(keep_b[:half], got_b[:half])
        else:
            keep_a, keep_b = summed_pair(keep_a, got_a), summed_pair(keep_b, got_b)
    both = jnp.concatenate([keep_a, keep_b], axis=1)
    rows = both.shape[0] // 4
    low, high = tail
    total = both[:rows].astype(f32)
    for k, mask in ((1, low), (2, high), (3, low | high)):
        total = total + swapped(both[k * rows : (k + 1) * rows], mask).astype(f32)
    return total


VMEM_BYTES = 56 << 20
TILE = 512


def norm_parts(values):
    average = jnp.mean(values, axis=-1, keepdims=True)
    centred = values - average
    variance = jnp.mean(centred * centred, axis=-1, keepdims=True)
    scale = lax.rsqrt(variance + norm_eps)
    return centred * scale, scale


def norm_back(unit, scale, gain, grad):
    inner = grad * gain
    shift = jnp.mean(inner, axis=-1, keepdims=True)
    along = jnp.mean(inner * unit, axis=-1, keepdims=True)
    return scale * (inner - shift - unit * along)


def mul(lhs, rhs):
    return jnp.dot(lhs, rhs, preferred_element_type=f32)


def mul_bt(lhs, rhs):
    return lax.dot_general(lhs, rhs, (((1,), (1,)), ((), ())), preferred_element_type=f32)


def mul_at(lhs, rhs):
    return lax.dot_general(lhs, rhs, (((0,), (0,)), ((), ())), preferred_element_type=f32)


def params(**more):
    return pltpu.CompilerParams(vmem_limit_bytes=VMEM_BYTES, **more)


def cost(flops, moved, transcendentals=0):
    return pl.CostEstimate(flops=flops, bytes_accessed=moved, transcendentals=transcendentals)


def lane_halves(dtype):
    lane = lax.broadcasted_iota(jnp.int32, (1, 2 * HEAD), 1)
    low = jnp.where(lane < HEAD, 1.0, 0.0)
    return low.astype(dtype), (1.0 - low).astype(dtype)


def two_heads(pair):
    low, high = lane_halves(bf16)
    return jnp.concatenate([pair * low, pair * high], axis=0)


def same_sequence(rows, row0, cols, col0, seq_len):
    row = (lax.broadcasted_iota(jnp.int32, (rows, cols), 0) + row0) // seq_len
    col = (lax.broadcasted_iota(jnp.int32, (rows, cols), 1) + col0) // seq_len
    return row == col


def masked_softmax(scores, mask):
    scores = jnp.where(mask, scores, -1e30)
    raised = jnp.exp(scores - jnp.max(scores, axis=-1, keepdims=True))
    return raised * (1.0 / jnp.sum(raised, axis=-1, keepdims=True))


def pair_cols(part, pair):
    start = part * D + pair * 2 * HEAD
    return slice(start, start + 2 * HEAD)


def front_kernel(
    seq_len, windows, ln_rows, x_ref, g1_ref, b1_ref, wqkv_ref, wo_ref, g2_ref, b2_ref, h1_ref,
    qkv_ref, att_ref, mid_ref, h2_ref, sum_ref
):
    rows = x_ref.shape[0]
    gain1, bias1 = g1_ref[...].astype(f32), b1_ref[...].astype(f32)
    gain2, bias2 = g2_ref[...].astype(f32), b2_ref[...].astype(f32)

    @pl.loop(0, rows // ln_rows)
    def _(step):
        at = pl.ds(pl.multiple_of(step * ln_rows, ln_rows), ln_rows)
        unit, _ = norm_parts(x_ref[at, :].astype(f32))
        h1_ref[at, :] = (unit * gain1 + bias1).astype(bf16)

    @pl.loop(0, 3 * D // 256)
    def _(step):
        at = pl.ds(pl.multiple_of(step * 256, 256), 256)
        qkv_ref[:, at] = mul(h1_ref[...], wqkv_ref[:, at]).astype(bf16)

    def attend(q_rows, k_rows, mask):
        for pair in range(HEADS // 2):
            queries = two_heads(qkv_ref[q_rows, pair_cols(0, pair)] * bf16(HEAD ** (-0.5)))
            scores = mul_bt(queries, qkv_ref[k_rows, pair_cols(1, pair)])
            probs = masked_softmax(scores, mask).astype(bf16)
            half = probs.shape[0] // 2
            vals = qkv_ref[k_rows, pair_cols(2, pair)]
            low, high = lane_halves(f32)
            mixed = mul(probs, vals)
            att_ref[q_rows, pair_cols(0, pair)] = (
                mixed[:half] * low + mixed[half:] * high
            ).astype(bf16)

    if len(windows) == 1:
        size = windows[0]
        one = same_sequence(size, 0, size, 0, seq_len)
        mask = jnp.concatenate([one, one], axis=0)

        @pl.loop(0, rows // size)
        def _(step):
            at = pl.ds(pl.multiple_of(step * size, size), size)
            attend(at, at, mask)
    else:
        for row0, count, key0, keys in windows:
            one = same_sequence(count, row0, keys, key0, seq_len)
            attend(pl.ds(row0, count), pl.ds(key0, keys), jnp.concatenate([one, one], axis=0))

    @pl.loop(0, D // 256)
    def _(step):
        at = pl.ds(pl.multiple_of(step * 256, 256), 256)
        mid_ref[:, at] = x_ref[:, at].astype(f32) + mul(att_ref[...], wo_ref[:, at])

    @pl.loop(0, rows // ln_rows)
    def _(step):
        at = pl.ds(pl.multiple_of(step * ln_rows, ln_rows), ln_rows)
        unit, _ = norm_parts(mid_ref[at, :])
        h2_ref[at, :] = (unit * gain2 + bias2).astype(bf16)

    if seq_len % 8 == 0:
        per = ln_rows // seq_len

        @pl.loop(0, rows // ln_rows)
        def _(step):
            values = mid_ref[pl.ds(pl.multiple_of(step * ln_rows, ln_rows), ln_rows), :]
            sum_ref[pl.ds(pl.multiple_of(step * per, per), per), :] = jnp.sum(
                values.reshape(per, seq_len, D), axis=1
            )
    else:
        for k in range(rows // seq_len):
            first, last = k * seq_len, (k + 1) * seq_len
            at8, end8 = first // 8 * 8, -(-last // 8) * 8
            values = mid_ref[at8:end8, :]
            place = lax.broadcasted_iota(jnp.int32, values.shape, 0) + at8
            inside = (place >= first) & (place < last)
            sum_ref[k : k + 1, :] = jnp.sum(
                jnp.where(inside, values, 0.0), axis=0, keepdims=True
            )


def front(seq_len, windows, ln_rows, rows_in, gain1, bias1, wqkv, wo, wo_col, gain2, bias2):
    rows = rows_in.shape[0]
    shapes = [
        ((rows, D), bf16),
        ((rows, 3 * D), bf16),
        ((rows, D), bf16),
        ((rows, D), f32),
        ((rows, D), bf16),
        ((rows // seq_len, D), f32),
    ]
    whole = lambda shape: pl.BlockSpec(shape, lambda i: (0, 0))
    row = whole((1, D))
    return pl.pallas_call(
        functools.partial(front_kernel, seq_len, windows, ln_rows),
        grid=(1,),
        out_shape=[jax.ShapeDtypeStruct(*item) for item in shapes],
        in_specs=[
            whole((rows, D)), row, row, whole((D, 3 * D)),
            pl.BlockSpec((D, D), lambda i: (0, wo_col)), row, row,
        ],
        out_specs=[whole(item[0]) for item in shapes],
        compiler_params=params(),
        cost_estimate=cost(rows * D * D * 8, 14 * D * rows + 8 * D * D, rows * 128 * HEADS),
        name="front",
    )(rows_in, gain1[None], bias1[None], wqkv, wo, gain2[None], bias2[None])


def gelu_parts(inner):
    half = 0.5 * (1.0 + lax.erf(inner * (0.5**0.5)))
    return inner * half, half


def pool_matrix(count, rows, row0, seq_len):
    row = (lax.broadcasted_iota(jnp.int32, (count, rows), 1) + row0) // seq_len
    return jnp.where(row == lax.broadcasted_iota(jnp.int32, (count, rows), 0), 1.0, 0.0).astype(bf16)


def two_terms(mean):
    high = mean.astype(bf16)
    low = (mean - high.astype(f32)).astype(bf16)
    return jnp.concatenate([high, low], axis=0)


def unit_rows(pooled):
    inverse = lax.rsqrt(jnp.sum(pooled * pooled, axis=-1, keepdims=True) + norm_eps)
    return pooled * inverse, inverse


def text_up_kernel(h2_ref, wu_ref, wd_ref, sum_ref, slope_ref, hid_ref, unit_ref, inv_ref, acc):
    step = pl.program_id(0)
    chunk = 128
    per = chunk // TXT_LEN
    pool = pool_matrix(per, chunk, 0, TXT_LEN)
    for k in range(h2_ref.shape[0] // chunk):
        inner = mul(h2_ref[k * chunk : (k + 1) * chunk, :], wu_ref[...])
        value, half = gelu_parts(inner)
        slope = half + inner * (jnp.exp(-0.5 * inner * inner) * 0.3989422804014327)
        slope_ref[k * chunk : (k + 1) * chunk, :] = slope.astype(bf16)
        hid_ref[k * per : (k + 1) * per, :] = mul(pool, value.astype(bf16))
    terms = mul(two_terms(hid_ref[...] * (1.0 / TXT_LEN)), wd_ref[...])
    count = hid_ref.shape[0]
    added = terms[:count] + terms[count:]

    @pl.when(step == 0)
    def _():
        acc[...] = sum_ref[...] * (1.0 / TXT_LEN) + added

    @pl.when(step > 0)
    def _():
        acc[...] += added

    @pl.when(step == pl.num_programs(0) - 1)
    def _():
        unit, inverse = unit_rows(acc[...])
        unit_ref[...] = unit
        inv_ref[...] = jnp.broadcast_to(inverse, inv_ref.shape)


def text_up(normed2, weight_up, weight_down, middle_sum):
    rows, count = normed2.shape[0], middle_sum.shape[0]
    fixed = lambda shape: pl.BlockSpec(shape, lambda i: (0, 0))
    return pl.pallas_call(
        text_up_kernel,
        grid=(FF // TILE,),
        out_shape=[
            jax.ShapeDtypeStruct((rows, FF), bf16),
            jax.ShapeDtypeStruct((count, FF), f32),
            jax.ShapeDtypeStruct((count, D), f32),
            jax.ShapeDtypeStruct((count, 128), f32),
        ],
        in_specs=[
            fixed((rows, D)),
            pl.BlockSpec((D, TILE), lambda i: (0, i)),
            pl.BlockSpec((TILE, D), lambda i: (i, 0)),
            fixed((count, D)),
        ],
        out_specs=[
            pl.BlockSpec((rows, TILE), lambda i: (0, i)),
            pl.BlockSpec((count, TILE), lambda i: (0, i)),
            fixed((count, D)),
            fixed((count, 128)),
        ],
        scratch_shapes=[pltpu.VMEM((count, D), f32)],
        compiler_params=params(),
        cost_estimate=cost(2 * rows * D * FF, 4 * D * FF + 2 * rows * FF, 20 * rows * FF),
        name="text_up",
    )(normed2, weight_up, weight_down, middle_sum)


def image_up_kernel(fold, h2_ref, wu_ref, wd_ref, sum_ref, out_ref, acc):
    step = pl.program_id(0)
    rows, count = h2_ref.shape[0], sum_ref.shape[0]
    chunk = 80
    summed = jnp.zeros((count, TILE), f32)
    for k in range(rows // chunk):
        inner = mul(h2_ref[k * chunk : (k + 1) * chunk, :], wu_ref[...])
        value, _ = gelu_parts(inner)
        pool = pool_matrix(count, chunk, k * chunk, IMG_LEN)
        summed = summed + mul(pool, value.astype(bf16))
    mean = two_terms(summed * (1.0 / IMG_LEN))
    place = lax.broadcasted_iota(jnp.int32, (TILE, TILE // fold), 0)
    picked = lax.broadcasted_iota(jnp.int32, (TILE, TILE // fold), 1) * fold
    terms = jnp.zeros((2 * count, D), f32)
    for k in range(fold):
        chosen = jnp.where(place == picked + k, 1.0, 0.0).astype(bf16)
        part = mul(mean, chosen).astype(bf16)
        terms = terms + mul(part, wd_ref[:, k * D : (k + 1) * D])
    added = terms[:count] + terms[count:]

    @pl.when(step == 0)
    def _():
        acc[...] = sum_ref[...] * (1.0 / IMG_LEN) + added

    @pl.when(step > 0)
    def _():
        acc[...] += added

    @pl.when(step == pl.num_programs(0) - 1)
    def _():
        out_ref[...] = unit_rows(acc[...])[0].astype(bf16)


def image_up(normed2, whole, up_col, down_col, middle_sum):
    rows, count = normed2.shape[0], middle_sum.shape[0]
    fold = FF // D
    fixed = lambda shape: pl.BlockSpec(shape, lambda i: (0, 0))
    return pl.pallas_call(
        functools.partial(image_up_kernel, fold),
        grid=(FF // TILE,),
        out_shape=jax.ShapeDtypeStruct((count, D), bf16),
        in_specs=[
            fixed((rows, D)),
            pl.BlockSpec((D, TILE), lambda i: (0, up_col // TILE + i)),
            pl.BlockSpec((TILE // fold, fold * D), lambda i: (i, down_col // (fold * D))),
            fixed((count, D)),
        ],
        out_specs=fixed((count, D)),
        scratch_shapes=[pltpu.VMEM((count, D), f32)],
        compiler_params=params(),
        cost_estimate=cost(2 * rows * D * FF, 4 * D * FF, 15 * rows * FF),
        name="image_up",
    )(normed2, whole, whole, middle_sum)


def loss_parts(text_rows, pos, image_all):
    similar = mul_bt(text_rows, image_all) * logit_scale
    shifted = jnp.exp(similar - logit_scale)
    alive = jnp.max(pos, axis=1, keepdims=True)
    row_sum = jnp.sum(shifted, axis=1, keepdims=True)
    row_count = jnp.maximum(jnp.sum(pos, axis=1, keepdims=True), 1.0)
    return similar, shifted, alive, row_sum, row_count


def sums_over_captions(text_rows, pos, image_all):
    similar, shifted, alive, row_sum, row_count = loss_parts(text_rows, pos, image_all)
    pos_similar = pos * similar
    cap_term = alive * (
        logit_scale + jnp.log(row_sum) - jnp.sum(pos_similar, axis=1, keepdims=True) / row_count
    )
    return (
        jnp.sum(alive * shifted, axis=0, keepdims=True),
        jnp.sum(pos, axis=0, keepdims=True),
        jnp.sum(pos_similar, axis=0, keepdims=True),
        jnp.sum(cap_term, axis=0, keepdims=True),
        jnp.sum(alive, axis=0, keepdims=True),
    )


def loss_from(sums):
    col_sum, col_count, col_pos, cap_total, live_total = sums
    img_term = logit_scale + jnp.log(col_sum) - col_pos / col_count
    return 0.5 * cap_total / live_total + 0.5 * jnp.mean(img_term, axis=1, keepdims=True)


def grad_of_unit(text_rows, pos, image_all, col_sum, col_count, live_total):
    _, shifted, alive, row_sum, row_count = loss_parts(text_rows, pos, image_all)
    cap_share, img_share = 0.5 / live_total, 0.5 / image_all.shape[0]
    grad_sims = alive * shifted * (cap_share / row_sum + img_share / col_sum) - pos * (
        cap_share / row_count + img_share / col_count
    )
    return mul(grad_sims.astype(bf16), image_all) * logit_scale


def turned(grad, unit):
    return grad - unit * jnp.sum(grad * unit, axis=-1, keepdims=True)


def loss_kernel(
    pack_ref, image_ref, own_ref, unit_ref, inv_ref, loss_ref, row_ref, col_sum_ref, col_count_ref,
    live_ref
):
    image_all = image_ref[...]
    chunk = 256
    total = None
    for k in range(pack_ref.shape[0] // chunk):
        at = slice(k * chunk, (k + 1) * chunk)
        part = sums_over_captions(pack_ref[at, :D], pack_ref[at, D:].astype(f32), image_all)
        total = part if total is None else [a + b for a, b in zip(total, part)]
    loss_ref[...] = jnp.broadcast_to(loss_from(total), loss_ref.shape)
    col_sum, col_count, _, _, live_total = total
    col_sum_ref[...] = col_sum
    col_count_ref[...] = col_count
    live_ref[...] = jnp.broadcast_to(live_total, live_ref.shape)
    grad = grad_of_unit(
        own_ref[:, :D], own_ref[:, D:].astype(f32), image_all, col_sum, col_count, live_total
    )
    row_ref[...] = inv_ref[:, :1] * turned(grad, unit_ref[...]) * (1.0 / TXT_LEN)


def loss_and_rows(pack, image_all, own_pack, unit, inverse):
    images, count = image_all.shape[0], own_pack.shape[0]
    shapes = [(1, 128), (count, D), (1, images), (1, images), (1, 128)]
    return pl.pallas_call(
        loss_kernel,
        out_shape=[jax.ShapeDtypeStruct(shape, f32) for shape in shapes],
        compiler_params=params(),
        cost_estimate=cost(2 * pack.shape[0] * images * D, 2 * pack.size, pack.shape[0] * images),
        name="loss_and_rows",
    )(pack, image_all, own_pack, unit, inverse)


def down_kernel(pack_ref, image_ref, col_sum_ref, col_count_ref, live_ref, hid_ref, out_ref):
    step = pl.program_id(0)
    text_rows = pack_ref[:, :D]
    grad = grad_of_unit(
        text_rows, pack_ref[:, D:].astype(f32), image_ref[...], col_sum_ref[...],
        col_count_ref[...], live_ref[:, :1]
    )
    rows = (turned(grad, text_rows.astype(f32)) * (1.0 / TXT_LEN)).astype(bf16)
    part = mul_at(hid_ref[...], rows)

    @pl.when(step == 0)
    def _():
        out_ref[...] = part

    @pl.when(step > 0)
    def _():
        out_ref[...] += part


def grad_of_down(pack, image_all, col_sum, col_count, live_total, hidden_cols):
    images, chunk = image_all.shape[0], 256
    fixed = lambda shape: pl.BlockSpec(shape, lambda i: (0, 0))
    per = hidden_cols.shape[1]
    return pl.pallas_call(
        down_kernel,
        grid=(pack.shape[0] // chunk,),
        out_shape=jax.ShapeDtypeStruct((per, D), f32),
        in_specs=[
            pl.BlockSpec((chunk, pack.shape[1]), lambda i: (i, 0)),
            fixed((images, D)), fixed((1, images)), fixed((1, images)), fixed((1, 128)),
            pl.BlockSpec((chunk, per), lambda i: (i, 0)),
        ],
        out_specs=fixed((per, D)),
        compiler_params=params(),
        cost_estimate=cost(4 * pack.shape[0] * images * D, 2 * pack.size, pack.shape[0] * images),
        name="grad_of_down",
    )(pack, image_all, col_sum, col_count, live_total, hidden_cols)


def mlp_back_kernel(
    low_ref, wd_ref, slope_ref, wu_ref, lhs_ref, mid_ref, gain_ref, row_ref, keep_a, send_a, keep_b,
    send_b, out_ref, gain_out, bias_out, acc
):
    step = pl.program_id(0)
    count, rows = low_ref.shape[0], slope_ref.shape[0]
    half = D // 2
    hidden = mul_bt(low_ref[...], wd_ref[...])
    wide = jnp.broadcast_to(hidden[:, None, :], (count, TXT_LEN, TILE)).reshape(rows, TILE)
    inner = (wide * slope_ref[...].astype(f32)).astype(bf16)
    weight = mul(lhs_ref[0], inner).astype(bf16)

    @pl.when(step < pl.num_programs(0) // 2)
    def _():
        keep_a[...] = weight[:half]
        send_a[...] = weight[half:]

    @pl.when(step >= pl.num_programs(0) // 2)
    def _():
        keep_b[...] = weight[:half]
        send_b[...] = weight[half:]

    added = mul_bt(inner, wu_ref[...])

    @pl.when(step == 0)
    def _():
        acc[...] = added

    @pl.when(step > 0)
    def _():
        acc[...] += added

    @pl.when(step == pl.num_programs(0) - 1)
    def _():
        chunk = 128
        per = chunk // TXT_LEN
        gain = gain_ref[...]
        gain_out[...] = jnp.zeros_like(gain_out)
        bias_out[...] = jnp.zeros_like(bias_out)

        @pl.loop(0, rows // chunk)
        def _(k):
            at = pl.ds(pl.multiple_of(k * chunk, chunk), chunk)
            unit, scale = norm_parts(mid_ref[at, :])
            grad = acc[at, :]
            gain_out[...] += jnp.sum(grad * unit, axis=0, keepdims=True)
            bias_out[...] += jnp.sum(grad, axis=0, keepdims=True)
            row = row_ref[pl.ds(pl.multiple_of(k * per, per), per), :]
            row = jnp.broadcast_to(row[:, None, :], (per, TXT_LEN, D)).reshape(chunk, D)
            out_ref[at, :] = row + norm_back(unit, scale, gain, grad)


def mlp_back(grad_row, weight_down, slope, weight_up, lhs, middle, gain):
    rows, count = slope.shape[0], grad_row.shape[0]
    steps = FF // TILE
    fixed = lambda shape: pl.BlockSpec(shape, lambda i: (0, 0))
    first = pl.BlockSpec((D // 2, TILE), lambda i: (0, jnp.minimum(i, steps // 2 - 1)))
    second = pl.BlockSpec((D // 2, TILE), lambda i: (0, jnp.maximum(i - steps // 2, 0)))
    part = jax.ShapeDtypeStruct((D // 2, FF // 2), bf16)
    line = jax.ShapeDtypeStruct((1, D), f32)
    return pl.pallas_call(
        mlp_back_kernel,
        grid=(steps,),
        out_shape=[part] * 4 + [jax.ShapeDtypeStruct((rows, D), f32), line, line],
        in_specs=[
            fixed((count, D)),
            pl.BlockSpec((TILE, D), lambda i: (i, 0)),
            pl.BlockSpec((rows, TILE), lambda i: (0, i)),
            pl.BlockSpec((D, TILE), lambda i: (0, i)),
            pl.BlockSpec((1, D, rows), lambda i: (i // (steps // 2), 0, 0)),
            fixed((rows, D)),
            fixed((1, D)),
            fixed((count, D)),
        ],
        out_specs=[first, first, second, second, fixed((rows, D)), fixed((1, D)), fixed((1, D))],
        scratch_shapes=[pltpu.VMEM((rows, D), f32)],
        compiler_params=params(),
        cost_estimate=cost(4 * rows * D * FF, 4 * D * FF + 2 * rows * FF + 2 * D * FF, rows * FF),
        name="mlp_back",
    )(grad_row.astype(bf16), weight_down, slope, weight_up, lhs, middle, gain[None], grad_row)


def attention_back_kernel(grad_ref, wo_ref, qkv_ref, low_ref, out_ref):
    rows, chunk = grad_ref.shape[0], 128
    one = same_sequence(chunk, 0, chunk, 0, TXT_LEN)
    mask = jnp.concatenate([one, one], axis=0)

    @pl.loop(0, rows // chunk)
    def _(step):
        at = pl.ds(pl.multiple_of(step * chunk, chunk), chunk)
        low_ref[at, :] = grad_ref[at, :].astype(bf16)

    @pl.loop(0, rows // chunk)
    def _(step):
        at = pl.ds(pl.multiple_of(step * chunk, chunk), chunk)
        grad_att = mul_bt(low_ref[at, :], wo_ref[...]).astype(bf16)
        for pair in range(HEADS // 2):
            queries = two_heads(qkv_ref[at, pair_cols(0, pair)] * bf16(HEAD ** (-0.5)))
            keys = qkv_ref[at, pair_cols(1, pair)]
            vals = qkv_ref[at, pair_cols(2, pair)]
            grads = two_heads(grad_att[:, pair_cols(0, pair)])
            probs = masked_softmax(mul_bt(queries, keys), mask)
            grad_probs = mul_bt(grads, vals)
            along = jnp.sum(grad_probs * probs, axis=-1, keepdims=True)
            grad_scores = (probs * (grad_probs - along)).astype(bf16)
            side = jnp.concatenate([grad_scores[:chunk], grad_scores[chunk:]], axis=1)
            grad_q = mul(side, two_heads(keys)) * HEAD ** (-0.5)
            grad_k = mul_at(grad_scores, queries)
            grad_v = mul_at(probs.astype(bf16), grads)
            out_ref[at, pair_cols(0, pair)] = grad_q.astype(bf16)
            out_ref[at, pair_cols(1, pair)] = grad_k.astype(bf16)
            out_ref[at, pair_cols(2, pair)] = grad_v.astype(bf16)


def attention_back(grad_middle, weight_out, project):
    rows = project.shape[0]
    return pl.pallas_call(
        attention_back_kernel,
        out_shape=[
            jax.ShapeDtypeStruct((rows, D), bf16),
            jax.ShapeDtypeStruct((rows, 3 * D), bf16),
        ],
        compiler_params=params(),
        cost_estimate=cost(2 * rows * D * D, 16 * rows * D + 2 * D * D, rows * 128 * HEADS),
        name="attention_back",
    )(grad_middle, weight_out, project)


def weight_back_kernel(lhs_ref, proj_ref, low_ref, keep_a, send_a, keep_b, send_b):
    step = pl.program_id(0)
    half = D // 2

    @pl.when(step < 2)
    def _():
        weight = mul(lhs_ref[0], proj_ref[...]).astype(bf16)
        keep_a[...] = weight[:half]
        send_a[...] = weight[half:]

    @pl.when(step == 2)
    def _():
        weight = mul(lhs_ref[0], proj_ref[...]).astype(bf16)
        keep_b[...] = weight[:half]
        send_b[...] = weight[half:]

    @pl.when(step == 3)
    def _():
        weight = mul(lhs_ref[0], low_ref[...]).astype(bf16)
        keep_b[...] = weight[:half]
        send_b[...] = weight[half:]


def weight_back(lhs, grad_proj, grad_low):
    rows = grad_proj.shape[0]
    first = pl.BlockSpec((D // 2, D), lambda i: (0, jnp.minimum(i, 1)))
    second = pl.BlockSpec((D // 2, D), lambda i: (0, jnp.maximum(i - 2, 0)))
    return pl.pallas_call(
        weight_back_kernel,
        grid=(4,),
        out_shape=[jax.ShapeDtypeStruct((D // 2, 2 * D), bf16)] * 4,
        in_specs=[
            pl.BlockSpec((1, D, rows), lambda i: (jnp.maximum(i - 1, 0), 0, 0)),
            pl.BlockSpec((rows, D), lambda i: (0, jnp.minimum(i, 2))),
            pl.BlockSpec((rows, D), lambda i: (0, 0)),
        ],
        out_specs=[first, first, second, second],
        compiler_params=params(),
        cost_estimate=cost(8 * rows * D * D, 8 * rows * D + 14 * D * D),
        name="weight_back",
    )(lhs, grad_proj, grad_low)


def input_back_kernel(proj_ref, w_ref, x_ref, gain_ref, mid_ref, out_ref, gain_out, bias_out, acc):
    step = pl.program_id(0)
    rows, chunk = x_ref.shape[0], 128
    added = mul_bt(proj_ref[...], w_ref[...])

    @pl.when(step == 0)
    def _():
        acc[...] = added

    @pl.when(step > 0)
    def _():
        acc[...] += added

    @pl.when(step == pl.num_programs(0) - 1)
    def _():
        gain = gain_ref[...]
        gain_out[...] = jnp.zeros_like(gain_out)
        bias_out[...] = jnp.zeros_like(bias_out)

        @pl.loop(0, rows // chunk)
        def _(k):
            at = pl.ds(pl.multiple_of(k * chunk, chunk), chunk)
            unit, scale = norm_parts(x_ref[at, :].astype(f32))
            grad = acc[at, :]
            gain_out[...] += jnp.sum(grad * unit, axis=0, keepdims=True)
            bias_out[...] += jnp.sum(grad, axis=0, keepdims=True)
            out_ref[at, :] = mid_ref[at, :] + norm_back(unit, scale, gain, grad)


def input_back(grad_proj, weight, rows_in, gain, grad_middle):
    rows = rows_in.shape[0]
    fixed = lambda shape: pl.BlockSpec(shape, lambda i: (0, 0))
    line = jax.ShapeDtypeStruct((1, D), f32)
    return pl.pallas_call(
        input_back_kernel,
        grid=(3,),
        out_shape=[jax.ShapeDtypeStruct((rows, D), f32), line, line],
        in_specs=[
            pl.BlockSpec((rows, D), lambda i: (0, i)),
            pl.BlockSpec((D, D), lambda i: (0, i)),
            fixed((rows, D)), fixed((1, D)), fixed((rows, D)),
        ],
        out_specs=[fixed((rows, D)), fixed((1, D)), fixed((1, D))],
        scratch_shapes=[pltpu.VMEM((rows, D), f32)],
        compiler_params=params(),
        cost_estimate=cost(6 * rows * D * D, 14 * rows * D + 6 * D * D),
        name="input_back",
    )(grad_proj, weight, rows_in, gain[None], grad_middle)


def local(
    images,
    captions,
    img_gain1,
    img_bias1,
    img_qkv,
    img_out,
    img_gain2,
    img_bias2,
    img_up,
    img_down,
    txt_gain1,
    txt_bias1,
    txt_qkv,
    txt_out,
    txt_gain2,
    txt_bias2,
    txt_up,
    txt_down,
    counts,
    matches,
):
    peers = lax.axis_size(AXIS)
    own = lax.axis_index(AXIS)
    per = D // peers
    img_local = counts.shape[0]
    cap_local = matches.shape[0]
    total_images = matches.shape[1]

    shard = jnp.concatenate(
        [
            img_qkv.reshape(per, 3 * D),
            img_out.reshape(per, D),
            img_up.reshape(per, FF),
            img_down.reshape(per, FF),
        ],
        axis=1,
    )
    whole = lax.all_gather(shard, AXIS, axis=0, tiled=True)

    normed1, project, attended, middle, normed2, middle_sum = front(
        TXT_LEN, (128,), 128, captions, txt_gain1, txt_bias1, txt_qkv, txt_out, 0, txt_gain2, txt_bias2
    )
    slope, hidden_sum, text_unit, inverse = text_up(normed2, txt_up, txt_down, middle_sum)
    text_low = text_unit.astype(bf16)

    ends_at = jnp.cumsum(counts)
    slot_ids = lax.iota(jnp.int32, cap_local)
    owner = jnp.sum((ends_at[None, :] <= slot_ids[:, None]).astype(jnp.int32), axis=1)
    owner = owner + own * img_local
    live = slot_ids < ends_at[-1]
    columns = lax.iota(jnp.int32, total_images)
    positive = ((matches > 0) | (owner[:, None] == columns[None, :])) & live[:, None]

    own_pack = jnp.concatenate([text_low, positive.astype(bf16)], axis=1)
    small = peers * cap_local * total_images <= 1 << 20
    if small:
        text_pack = gathered(own_pack).reshape(-1, D + total_images)
        hidden_cols = lax.all_to_all(
            (hidden_sum * inverse[:, :1]).astype(bf16), AXIS, split_axis=1, concat_axis=0, tiled=True
        )

    windows = ((0, 208, 0, 256), (208, 192, 192, 208))
    image_front = front(
        IMG_LEN, windows, 80, images, img_gain1, img_bias1, whole, whole, 3, img_gain2, img_bias2
    )
    image_low = image_up(image_front[4], whole, 4 * D, 4 * D + FF, image_front[5])
    image_all = spread(image_low).reshape(total_images, D)

    order_a, order_b, tail = stage_orders()
    matrix_a, matrix_b = row_order(order_a, tail), row_order(order_b, tail)
    lhs_up = jnp.stack([placed(matrix_a, normed2), placed(matrix_b, normed2)])
    lhs_rest = jnp.stack(
        [placed(matrix_a, normed1), placed(matrix_b, normed1), placed(matrix_b, attended)]
    )

    if small:
        loss_value, grad_row, col_sum, col_count, live_total = loss_and_rows(
            text_pack, image_all, own_pack, text_unit, inverse
        )
        loss_value = loss_value[0, 0]
    else:
        pos = own_pack[:, D:].astype(f32)
        sums = lax.psum(sums_over_captions(text_low, pos, image_all), AXIS)
        loss_value = loss_from(sums)[0, 0]
        grad = grad_of_unit(text_low, pos, image_all, sums[0], sums[1], sums[4])
        grad_row = inverse[:, :1] * turned(grad, text_unit) * (1.0 / TXT_LEN)

    *up_parts, grad_middle, gain_two, bias_two = mlp_back(
        grad_row, txt_down, slope, txt_up, lhs_up, middle, txt_gain2
    )
    up_share = scattered(*up_parts)
    if small:
        grad_down = grad_of_down(text_pack, image_all, col_sum, col_count, live_total, hidden_cols)
    else:
        grad_down = lax.psum_scatter(
            mul_at(hidden_sum.astype(bf16), grad_row.astype(bf16)),
            AXIS,
            scatter_dimension=0,
            tiled=True,
        )
    grad_low, grad_proj = attention_back(grad_middle, txt_out, project)
    rest_share = scattered(*weight_back(lhs_rest, grad_proj, grad_low))
    caption_grad, gain_one, bias_one = input_back(
        grad_proj, txt_qkv, captions, txt_gain1, grad_middle
    )
    norms = jnp.concatenate([gain_one, bias_one, gain_two, bias_two], axis=0)
    norms = jnp.sum(spread(norms[None]), axis=0).reshape(4, D)
    return (
        loss_value,
        caption_grad,
        norms[0],
        norms[1],
        rest_share[:, : 3 * D].reshape(-1),
        rest_share[:, 3 * D :].reshape(-1),
        norms[2],
        norms[3],
        up_share.reshape(-1),
        grad_down.reshape(-1),
    )


def solution(mesh):
    split, flat, whole = P("blk", None), P("blk"), P()
    image_block = (whole, whole, flat, flat, whole, whole, flat, flat)
    return jax.shard_map(
        local,
        mesh=mesh,
        in_specs=(split, split) + image_block + (whole,) * 8 + (flat, split),
        out_specs=(whole, split, whole, whole, flat, flat, whole, whole, flat, flat),
        check_vma=False,
    )
```

profile of v0, /device:TPU:0, one launch (start us, length us, event | category | flops | bytes accessed | tf_op | source)
XLA Modules:
  0.0 345.2 jit_solution(12533664659882102444)
XLA Ops:
  15.1 18.7 %front.2 = (bf16[640,768]{1,0:T(8,128)(2,1)}, bf16[640,2304]{1,0:T(8,128)(2,1)}, bf16[640,768]{1,0:T(8,128)(2,1)}, f32[640,768]{1,0:T(8,128)}, bf16[640,768]{1,0:T(8,128)(2,1)}, /*index=5*/f32[40,768]{1,0:T(8,128)}) custom-call(bf16[640,768]{1,0:T(8,128)(2,1)} %x_ref.5, f32[1,768]{1,0:T(1,128)} %broadcast_in_dim.22.g1_ref.gain_ref, ...), custom_call_target="tpu_custom_call" | custom-call | flops 3019898880 | bytes 11599872 | tf_op jit(solution)/shard_map/front/pallas_call | solution.py:263
  33.8 13.8 %text_up.1 = (bf16[640,3072]{1,0:T(8,128)(2,1)}, f32[40,3072]{1,0:T(8,128)}, f32[40,768]{1,0:T(8,128)}, f32[40,128]{1,0:T(8,128)}) custom-call(bf16[640,768]{1,0:T(8,128)(2,1)} %get-tuple-element.43.h2_ref, bf16[768,3072]{1,0:T(8,128)(2,1)} %wu_ref.3, bf16[3072,768]{1,0:T(8,128)(2,1)} %wd_ref.3, f32[40,768]{1,0:T(8,128)} %get-tuple-element.44.sum_ref), custom_call_target="tpu_custom_call" | custom-call | flops 3019898880 | bytes 13369344 | tf_op jit(solution)/shard_map/text_up/pallas_call | solution.py:332
  49.9 4.1 %collective-permute-start = (bf16[1,40,1024]{2,1,0:T(8,128)(2,1)S(1)}, bf16[1,40,1024]{2,1,0:T(8,128)(2,1)S(1)}, u32[]{:S(2)}, u32[]{:S(2)}) collective-permute-start(bf16[1,40,1024]{2,1,0:T(8,128)(2,1)S(1)} %get-tuple-element.105), channel_id=1, source_target_pairs={{0,16},{1,17},{2,18},{3,19},{4,20},{5,21},{6,22},{7,23},{8,24},{9,... | collective-permute-start | bytes 245768 | tf_op jit(solution)/shard_map/ppermute | solution.py:26
  54.0 8.5 %collective-permute-done = bf16[1,40,1024]{2,1,0:T(8,128)(2,1)S(1)} collective-permute-done((bf16[1,40,1024]{2,1,0:T(8,128)(2,1)S(1)}, bf16[1,40,1024]{2,1,0:T(8,128)(2,1)S(1)}, u32[]{:S(2)}, u32[]{:S(2)}) %collective-permute-start) | collective-permute-done | bytes 81952 | tf_op jit(solution)/shard_map/ppermute | solution.py:26
  62.7 9.2 %collective-permute-done.1 = bf16[2,40,1024]{2,1,0:T(8,128)(2,1)S(1)} collective-permute-done((bf16[2,40,1024]{2,1,0:T(8,128)(2,1)S(1)}, bf16[2,40,1024]{2,1,0:T(8,128)(2,1)S(1)}, u32[]{:S(2)}, u32[]{:S(2)}) %collective-permute-start.1) | collective-permute-done | bytes 163872 | tf_op jit(solution)/shard_map/ppermute | solution.py:26
  78.0 10.0 %collective-permute-done.2 = bf16[4,40,1024]{2,1,0:T(8,128)(2,1)S(1)} collective-permute-done((bf16[4,40,1024]{2,1,0:T(8,128)(2,1)S(1)}, bf16[4,40,1024]{2,1,0:T(8,128)(2,1)S(1)}, u32[]{:S(2)}, u32[]{:S(2)}) %collective-permute-start.2) | collective-permute-done | bytes 327712 | tf_op jit(solution)/shard_map/ppermute | solution.py:26
  93.6 3.5 %fusion.12 = bf16[1,768,640]{2,1,0:T(8,128)(2,1)} fusion(bf16[640,768]{1,0:T(8,128)(2,1)} %get-tuple-element.43.h2_ref, s32[768]{0:T(1024)S(1)} %get-tuple-element.106), kind=kOutput, calls=%fused_computation.17 | convolution fusion | flops 756056064 | bytes 1969152 | tf_op jit(solution)/shard_map/dot_general | solution.py:130
  99.2 16.5 %collective-permute-done.3 = bf16[8,40,1024]{2,1,0:T(8,128)(2,1)S(1)} collective-permute-done((bf16[8,40,1024]{2,1,0:T(8,128)(2,1)S(1)}, bf16[8,40,1024]{2,1,0:T(8,128)(2,1)S(1)}, u32[]{:S(2)}, u32[]{:S(2)}) %collective-permute-start.3) | collective-permute-done | bytes 655392 | tf_op jit(solution)/shard_map/ppermute | solution.py:26
  117.8 16.7 %all-gather.2.cloned.1.call-done.wqkv_ref.wo_ref.wu_ref.wd_ref = bf16[768,9216]{1,0:T(8,128)(2,1)} async-done(((bf16[24,9216]{1,0:T(8,128)(2,1)}), bf16[768,9216]{1,0:T(8,128)(2,1)}) %all-gather.2.cloned.1.call-update) | async-done | bytes 14155792 | tf_op jit(solution)/shard_map/all_gather | solution.py:790
  134.5 13.8 %front.3 = (bf16[400,768]{1,0:T(8,128)(2,1)}, bf16[400,2304]{1,0:T(8,128)(2,1)}, bf16[400,768]{1,0:T(8,128)(2,1)}, f32[400,768]{1,0:T(8,128)}, bf16[400,768]{1,0:T(8,128)(2,1)}, /*index=5*/f32[8,768]{1,0:T(8,128)}) custom-call(bf16[400,768]{1,0:T(8,128)(2,1)} %x_ref.4, bf16[1,768]{1,0:T(2,128)(2,1)} %broadcast_in_dim.54.g1_ref, ...), custom_call_target="tpu_custom_call" | custom-call | flops 1887436800 | bytes 9019392 | tf_op jit(solution)/shard_map/front/pallas_call | solution.py:263
  148.3 14.1 %image_up.1 = bf16[8,768]{1,0:T(8,128)(2,1)} custom-call(bf16[400,768]{1,0:T(8,128)(2,1)} %get-tuple-element.46.h2_ref, bf16[768,9216]{1,0:T(8,128)(2,1)} %all-gather.2.cloned.1.call-done.wqkv_ref.wo_ref.wu_ref.wd_ref, bf16[768,9216]{1,0:T(8,128)(2,1)} %all-gather.2.cloned.1.call-done.wqkv_ref.wo_ref.wu_ref.wd_ref, f32[8,768]{1,0:T(8,128)} %get-tuple-element.47.sum_ref), custom_call_target="tpu_custom_call" | custom-call | flops 1887436800 | bytes 9437184 | tf_op jit(solution)/shard_map/image_up/pallas_call | solution.py:397
  171.8 3.7 %pad_maximum_fusion.lhs_ref = bf16[3,768,640]{2,1,0:T(8,128)(2,1)} fusion(bf16[1,768,640]{2,1,0:T(8,128)(2,1)} %fusion.10, bf16[1,768,640]{2,1,0:T(8,128)(2,1)} %fusion.11, bf16[1,768,640]{2,1,0:T(8,128)(2,1)} %fusion.13), kind=kLoop, calls=%fused_computation | loop fusion | flops 2949120 | bytes 5898240 | tf_op jit(solution)/shard_map/stack | solution.py:824
  179.9 3.9 %all-to-all-start.2 = ((bf16[40,32,96]{2,0,1:T(8,128)(2,1)}), bf16[40,32,96]{2,0,1:T(8,128)(2,1)S(1)}, u32[]{:S(2)}, u32[]{:S(2)}) async-start(bf16[40,32,96]{2,0,1:T(8,128)(2,1)} %copy.57), calls=%async_computation.2 | async-start | bytes 655360 | tf_op jit(solution)/shard_map/all_to_all | solution.py:810
  183.7 4.0 %loss_and_rows.1 = (f32[1,128]{1,0:T(1,128)}, f32[40,768]{1,0:T(8,128)}, f32[1,256]{1,0:T(1,128)}, f32[1,256]{1,0:T(1,128)}, f32[1,128]{1,0:T(1,128)}) custom-call(bf16[1280,1024]{1,0:T(8,128)(2,1)} %bitcast.68, bf16[256,768]{1,0:T(8,128)(2,1)} %bitcast.72, bf16[40,1024]{1,0:T(8,128)(2,1)} %get-tuple-element.104.own_ref, ...), custom_call_target="tpu_custom_call" | custom-call | flops 503316480 | bytes 2621440 | tf_op jit(solution)/shard_map/loss_and_rows/pallas_call | solution.py:483
  189.3 21.4 %mlp_back.1 = (bf16[384,1536]{1,0:T(8,128)(2,1)}, bf16[384,1536]{1,0:T(8,128)(2,1)}, bf16[384,1536]{1,0:T(8,128)(2,1)}, bf16[384,1536]{1,0:T(8,128)(2,1)}, f32[6...) custom-call(bf16[40,768]{1,0:T(8,128)(2,1)} %convert_element_type.239.low_ref, bf16[3072,768]{1,0:T(8,128)(2,1)} %wd_ref.3, ...), custom_call_target="tpu_custom_call" | custom-call | flops 6039797760 | bytes 18087936 | tf_op jit(solution)/shard_map/mlp_back/pallas_call | solution.py:591
  210.7 21.4 %attention_back.1 = (bf16[640,768]{1,0:T(8,128)(2,1)}, bf16[640,2304]{1,0:T(8,128)(2,1)}) custom-call(f32[640,768]{1,0:T(8,128)} %get-tuple-element.53.grad_ref.mid_ref, bf16[768,768]{1,0:T(8,128)(2,1)} %wo_ref.3, bf16[640,2304]{1,0:T(8,128)(2,1)} %get-tuple-element.54.qkv_ref), custom_call_target="tpu_custom_call" | custom-call | flops 754974720 | bytes 9043968 | tf_op jit(solution)/shard_map/attention_back/pallas_call | solution.py:647
  232.1 8.7 %weight_back.1 = (bf16[384,1536]{1,0:T(8,128)(2,1)}, bf16[384,1536]{1,0:T(8,128)(2,1)}, bf16[384,1536]{1,0:T(8,128)(2,1)}, bf16[384,1536]{1,0:T(8,128)(2,1)}) custom-call(bf16[3,768,640]{2,1,0:T(8,128)(2,1)} %pad_maximum_fusion.lhs_ref, bf16[640,2304]{1,0:T(8,128)(2,1)} %get-tuple-element.55.proj_ref, bf16[640,768]{1,0:T(8,128)(2,1)} %get-tuple-element.63.low_ref), custom_call_target="tpu_custom_call" | custom-call | flops 3019898880 | bytes 12189696 | tf_op jit(solution)/shard_map/weight_back/pallas_call | solution.py:686
  241.1 9.4 %input_back.1 = (f32[640,768]{1,0:T(8,128)}, f32[1,768]{1,0:T(1,128)}, f32[1,768]{1,0:T(1,128)}) custom-call(bf16[640,2304]{1,0:T(8,128)(2,1)} %get-tuple-element.55.proj_ref, bf16[768,2304]{1,0:T(8,128)(2,1)} %w_ref.1, bf16[640,768]{1,0:T(8,128)(2,1)} %x_ref.5, f32[1,768]{1,0:T(1,128)} %broadcast_in_dim.22.g1_ref.gain_ref, ...), custom_call_target="tpu_custom_call" | custom-call | flops 2264924160 | bytes 10420224 | tf_op jit(solution)/shard_map/input_back/pallas_call | solution.py:735
  252.1 6.0 %all-to-all-start.1 = ((f32[32,1,4,768]{3,2,1,0:T(4,128)}), f32[32,1,4,768]{3,2,1,0:T(4,128)S(1)}, u32[]{:S(2)}, u32[]{:S(2)}) async-start(f32[32,1,4,768]{3,2,1,0:T(4,128)} %broadcast_in_dim.59), calls=%async_computation.1 | async-start | bytes 786432 | tf_op jit(solution)/shard_map/all_to_all | solution.py:49
  258.6 8.0 %grad_of_down.1 = f32[96,768]{1,0:T(8,128)} custom-call(bf16[1280,1024]{1,0:T(8,128)(2,1)} %bitcast.69, bf16[256,768]{1,0:T(8,128)(2,1)} %bitcast.73, f32[1,256]{1,0:T(1,128)} %get-tuple-element.72.col_sum_ref, f32[1,256]{1,0:T(1,128)} %get-tuple-element.73.col_count_ref, f32[1,128]{1,0:T(1,128)} %get-tuple-element.74.live_ref, bf16[1280,96]{1,0:T(8,128)(2,1)} %bitcast.75), custom_call_target="tpu_custom_call" | custom-call | flops 1006632960 | bytes 2621440 | tf_op jit(solution)/shard_map/grad_of_down/pallas_call | solution.py:515
  281.1 7.2 %collective-permute-done.6 = bf16[192,1536]{1,0:T(8,128)(2,1)S(1)} collective-permute-done((bf16[192,1536]{1,0:T(8,128)(2,1)S(1)}, bf16[192,1536]{1,0:T(8,128)(2,1)S(1)}, u32[]{:S(2)}, u32[]{:S(2)}) %collective-permute-start.6) | collective-permute-done | bytes 589856 | tf_op jit(solution)/shard_map/ppermute | solution.py:26
  292.2 8.8 %collective-permute-done.15 = bf16[192,1536]{1,0:T(8,128)(2,1)S(1)} collective-permute-done((bf16[192,1536]{1,0:T(8,128)(2,1)S(1)}, bf16[192,1536]{1,0:T(8,128)(2,1)S(1)}, u32[]{:S(2)}, u32[]{:S(2)}) %collective-permute-start.15) | collective-permute-done | bytes 589856 | tf_op jit(solution)/shard_map/ppermute | solution.py:26
  304.8 5.1 %collective-permute-done.7 = bf16[96,1536]{1,0:T(8,128)(2,1)S(1)} collective-permute-done((bf16[96,1536]{1,0:T(8,128)(2,1)S(1)}, bf16[96,1536]{1,0:T(8,128)(2,1)S(1)}, u32[]{:S(2)}, u32[]{:S(2)}) %collective-permute-start.7) | collective-permute-done | bytes 294944 | tf_op jit(solution)/shard_map/ppermute | solution.py:26
  320.2 13.1 %collective-permute-done.12 = bf16[24,3072]{1,0:T(8,128)(2,1)S(1)} collective-permute-done((bf16[24,3072]{1,0:T(8,128)(2,1)S(1)}, bf16[24,3072]{1,0:T(8,128)(2,1)S(1)}, u32[]{:S(2)}, u32[]{:S(2)}) %collective-permute-start.12) | collective-permute-done | bytes 147488 | tf_op jit(solution)/shard_map/ppermute | solution.py:26
  (162 shorter events, 81.4 us)
Async XLA Ops:
  7.2 127.3 %all-gather.2.cloned.1.call-start = ((), (), s32[]{:S(2)}) async-start(), calls=%async_computation.3 | async-start | bytes 14598144 | tf_op jit(solution)/shard_map/all_gather | solution.py:790
  49.9 12.6 %collective-permute-start = (bf16[1,40,1024]{2,1,0:T(8,128)(2,1)S(1)}, bf16[1,40,1024]{2,1,0:T(8,128)(2,1)S(1)}, u32[]{:S(2)}, u32[]{:S(2)}) collective-permute-start(bf16[1,40,1024]{2,1,0:T(8,128)(2,1)S(1)} %get-tuple-element.105), channel_id=1, source_target_pairs={{0,16},{1,17},{2,18},{3,19},{4,20},{5,21},{6,22},{7,23},{8,24},{9,... | collective-permute-start | bytes 245768 | tf_op jit(solution)/shard_map/ppermute | solution.py:26
  72.1 15.9 %collective-permute-start.2 = (bf16[4,40,1024]{2,1,0:T(8,128)(2,1)S(1)}, bf16[4,40,1024]{2,1,0:T(8,128)(2,1)S(1)}, u32[]{:S(2)}, u32[]{:S(2)}) collective-permute-start(bf16[4,40,1024]{2,1,0:T(8,128)(2,1)S(1)} %bitcast.74), channel_id=1, source_target_pairs={{0,4},{1,5},{2,6},{3,7},{4,0},{5,1},{6,2},{7,3},{8,12},{9,13},{10,... | collective-permute-start | bytes 983048 | tf_op jit(solution)/shard_map/ppermute | solution.py:26
  88.1 27.6 %collective-permute-start.3 = (bf16[8,40,1024]{2,1,0:T(8,128)(2,1)S(1)}, bf16[8,40,1024]{2,1,0:T(8,128)(2,1)S(1)}, u32[]{:S(2)}, u32[]{:S(2)}) collective-permute-start(bf16[8,40,1024]{2,1,0:T(8,128)(2,1)S(1)} %bitcast.71), channel_id=1, source_target_pairs={{0,2},{1,3},{2,0},{3,1},{4,6},{5,7},{6,4},{7,5},{8,10},{9,11},{10,... | collective-permute-start | bytes 1966088 | tf_op jit(solution)/shard_map/ppermute | solution.py:26
  116.1 59.4 %collective-permute-start.4 = (bf16[16,40,1024]{2,1,0:T(8,128)(2,1)S(1)}, bf16[16,40,1024]{2,1,0:T(8,128)(2,1)S(1)}, u32[]{:S(2)}, u32[]{:S(2)}) collective-permute-start(bf16[16,40,1024]{2,1,0:T(8,128)(2,1)S(1)} %bitcast.70), channel_id=1, source_target_pairs={{0,1},{1,0},{2,3},{3,2},{4,5},{5,4},{6,7},{7,6},{8,9},{9,8},{10,11... | collective-permute-start | bytes 3932168 | tf_op jit(solution)/shard_map/ppermute | solution.py:26
  163.9 16.0 %all-to-all-start = ((bf16[32,8,768]{2,1,0:T(8,128)(2,1)}), bf16[32,8,768]{2,1,0:T(8,128)(2,1)S(1)}, u32[]{:S(2)}, u32[]{:S(2)}) async-start(bf16[32,8,768]{2,1,0:T(8,128)(2,1)} %broadcast_in_dim.58), calls=%async_computation | async-start | bytes 786432 | tf_op jit(solution)/shard_map/all_to_all | solution.py:49
  179.9 71.3 %all-to-all-start.2 = ((bf16[40,32,96]{2,0,1:T(8,128)(2,1)}), bf16[40,32,96]{2,0,1:T(8,128)(2,1)S(1)}, u32[]{:S(2)}, u32[]{:S(2)}) async-start(bf16[40,32,96]{2,0,1:T(8,128)(2,1)} %copy.57), calls=%async_computation.2 | async-start | bytes 655360 | tf_op jit(solution)/shard_map/all_to_all | solution.py:810
  240.8 30.9 %collective-permute-start.5 = (bf16[384,1536]{1,0:T(8,128)(2,1)}, bf16[384,1536]{1,0:T(8,128)(2,1)S(1)}, u32[]{:S(2)}, u32[]{:S(2)}) collective-permute-start(bf16[384,1536]{1,0:T(8,128)(2,1)} %get-tuple-element.65), channel_id=1, source_target_pairs={{0,1},{1,0},{2,3},{3,2},{4,5},{5,4},{6,7},{7,6},{8,9},{9,8},{10,11... | collective-permute-start | bytes 3538952 | tf_op jit(solution)/shard_map/ppermute | solution.py:26
  252.1 18.9 %all-to-all-start.1 = ((f32[32,1,4,768]{3,2,1,0:T(4,128)}), f32[32,1,4,768]{3,2,1,0:T(4,128)S(1)}, u32[]{:S(2)}, u32[]{:S(2)}) async-start(f32[32,1,4,768]{3,2,1,0:T(4,128)} %broadcast_in_dim.59), calls=%async_computation.1 | async-start | bytes 786432 | tf_op jit(solution)/shard_map/all_to_all | solution.py:49
  258.0 14.5 %collective-permute-start.8 = (bf16[384,1536]{1,0:T(8,128)(2,1)}, bf16[384,1536]{1,0:T(8,128)(2,1)}, u32[]{:S(2)}, u32[]{:S(2)}) collective-permute-start(bf16[384,1536]{1,0:T(8,128)(2,1)} %get-tuple-element.67), channel_id=1, source_target_pairs={{0,1},{1,0},{2,3},{3,2},{4,5},{5,4},{6,7},{7,6},{8,9},{9,8},{10,11... | collective-permute-start | bytes 3538952 | tf_op jit(solution)/shard_map/ppermute | solution.py:26
  258.1 17.6 %collective-permute-start.14 = (bf16[384,1536]{1,0:T(8,128)(2,1)}, bf16[384,1536]{1,0:T(8,128)(2,1)}, u32[]{:S(2)}, u32[]{:S(2)}) collective-permute-start(bf16[384,1536]{1,0:T(8,128)(2,1)} %get-tuple-element.69), channel_id=1, source_target_pairs={{0,1},{1,0},{2,3},{3,2},{4,5},{5,4},{6,7},{7,6},{8,9},{9,8},{10,11... | collective-permute-start | bytes 3538952 | tf_op jit(solution)/shard_map/ppermute | solution.py:26
  268.3 10.2 %collective-permute-start.17 = (bf16[384,1536]{1,0:T(8,128)(2,1)}, bf16[384,1536]{1,0:T(8,128)(2,1)}, u32[]{:S(2)}, u32[]{:S(2)}) collective-permute-start(bf16[384,1536]{1,0:T(8,128)(2,1)} %get-tuple-element.71), channel_id=1, source_target_pairs={{0,1},{1,0},{2,3},{3,2},{4,5},{5,4},{6,7},{7,6},{8,9},{9,8},{10,11... | collective-permute-start | bytes 3538952 | tf_op jit(solution)/shard_map/ppermute | solution.py:26
  272.0 16.3 %collective-permute-start.6 = (bf16[192,1536]{1,0:T(8,128)(2,1)S(1)}, bf16[192,1536]{1,0:T(8,128)(2,1)S(1)}, u32[]{:S(2)}, u32[]{:S(2)}) collective-permute-start(bf16[192,1536]{1,0:T(8,128)(2,1)S(1)} %get-tuple-element.87), channel_id=1, source_target_pairs={{0,2},{1,3},{2,0},{3,1},{4,6},{5,7},{6,4},{7,5},{8,10},{9,11},{10,... | collective-permute-start | bytes 1769480 | tf_op jit(solution)/shard_map/ppermute | solution.py:26
  274.6 16.3 %collective-permute-start.9 = (bf16[192,1536]{1,0:T(8,128)(2,1)S(1)}, bf16[192,1536]{1,0:T(8,128)(2,1)S(1)}, u32[]{:S(2)}, u32[]{:S(2)}) collective-permute-start(bf16[192,1536]{1,0:T(8,128)(2,1)S(1)} %get-tuple-element.89), channel_id=1, source_target_pairs={{0,4},{1,5},{2,6},{3,7},{4,0},{5,1},{6,2},{7,3},{8,12},{9,13},{10,... | collective-permute-start | bytes 1769480 | tf_op jit(solution)/shard_map/ppermute | solution.py:26
  277.4 23.6 %collective-permute-start.15 = (bf16[192,1536]{1,0:T(8,128)(2,1)S(1)}, bf16[192,1536]{1,0:T(8,128)(2,1)S(1)}, u32[]{:S(2)}, u32[]{:S(2)}) collective-permute-start(bf16[192,1536]{1,0:T(8,128)(2,1)S(1)} %get-tuple-element.83), channel_id=1, source_target_pairs={{0,2},{1,3},{2,0},{3,1},{4,6},{5,7},{6,4},{7,5},{8,10},{9,11},{10,... | collective-permute-start | bytes 1769480 | tf_op jit(solution)/shard_map/ppermute | solution.py:26
  280.0 23.5 %collective-permute-start.18 = (bf16[192,1536]{1,0:T(8,128)(2,1)S(1)}, bf16[192,1536]{1,0:T(8,128)(2,1)S(1)}, u32[]{:S(2)}, u32[]{:S(2)}) collective-permute-start(bf16[192,1536]{1,0:T(8,128)(2,1)S(1)} %get-tuple-element.85), channel_id=1, source_target_pairs={{0,4},{1,5},{2,6},{3,7},{4,0},{5,1},{6,2},{7,3},{8,12},{9,13},{10,... | collective-permute-start | bytes 1769480 | tf_op jit(solution)/shard_map/ppermute | solution.py:26
  288.4 21.5 %collective-permute-start.7 = (bf16[96,1536]{1,0:T(8,128)(2,1)S(1)}, bf16[96,1536]{1,0:T(8,128)(2,1)S(1)}, u32[]{:S(2)}, u32[]{:S(2)}) collective-permute-start(bf16[96,1536]{1,0:T(8,128)(2,1)S(1)} %add_convert_fusion.18), channel_id=1, source_target_pairs={{0,4},{1,5},{2,6},{3,7},{4,0},{5,1},{6,2},{7,3},{8,12},{9,13},{10,... | collective-permute-start | bytes 884744 | tf_op jit(solution)/shard_map/ppermute | solution.py:26
  291.0 19.0 %collective-permute-start.10 = (bf16[96,1536]{1,0:T(8,128)(2,1)S(1)}, bf16[96,1536]{1,0:T(8,128)(2,1)S(1)}, u32[]{:S(2)}, u32[]{:S(2)}) collective-permute-start(bf16[96,1536]{1,0:T(8,128)(2,1)S(1)} %add_convert_fusion.15), channel_id=1, source_target_pairs={{0,2},{1,3},{2,0},{3,1},{4,6},{5,7},{6,4},{7,5},{8,10},{9,11},{10,... | collective-permute-start | bytes 884744 | tf_op jit(solution)/shard_map/ppermute | solution.py:26
  301.0 13.9 %collective-permute-start.16 = (bf16[96,1536]{1,0:T(8,128)(2,1)S(1)}, bf16[96,1536]{1,0:T(8,128)(2,1)S(1)}, u32[]{:S(2)}, u32[]{:S(2)}) collective-permute-start(bf16[96,1536]{1,0:T(8,128)(2,1)S(1)} %add_convert_fusion.12), channel_id=1, source_target_pairs={{0,4},{1,5},{2,6},{3,7},{4,0},{5,1},{6,2},{7,3},{8,12},{9,13},{10,... | collective-permute-start | bytes 884744 | tf_op jit(solution)/shard_map/ppermute | solution.py:26
  303.6 11.5 %collective-permute-start.19 = (bf16[96,1536]{1,0:T(8,128)(2,1)S(1)}, bf16[96,1536]{1,0:T(8,128)(2,1)S(1)}, u32[]{:S(2)}, u32[]{:S(2)}) collective-permute-start(bf16[96,1536]{1,0:T(8,128)(2,1)S(1)} %add_convert_fusion.9), channel_id=1, source_target_pairs={{0,2},{1,3},{2,0},{3,1},{4,6},{5,7},{6,4},{7,5},{8,10},{9,11},{10,... | collective-permute-start | bytes 884744 | tf_op jit(solution)/shard_map/ppermute | solution.py:26
  312.2 21.0 %collective-permute-start.12 = (bf16[24,3072]{1,0:T(8,128)(2,1)S(1)}, bf16[24,3072]{1,0:T(8,128)(2,1)S(1)}, u32[]{:S(2)}, u32[]{:S(2)}) collective-permute-start(bf16[24,3072]{1,0:T(8,128)(2,1)S(1)} %get-tuple-element.99), channel_id=1, source_target_pairs={{0,16},{1,17},{2,18},{3,19},{4,20},{5,21},{6,22},{7,23},{8,24},{9,... | collective-permute-start | bytes 442376 | tf_op jit(solution)/shard_map/ppermute | solution.py:26
  315.2 19.5 %collective-permute-start.20 = (bf16[24,3072]{1,0:T(8,128)(2,1)S(1)}, bf16[24,3072]{1,0:T(8,128)(2,1)S(1)}, u32[]{:S(2)}, u32[]{:S(2)}) collective-permute-start(bf16[24,3072]{1,0:T(8,128)(2,1)S(1)} %get-tuple-element.94), channel_id=1, source_target_pairs={{0,8},{1,9},{2,10},{3,11},{4,12},{5,13},{6,14},{7,15},{8,0},{9,1},... | collective-permute-start | bytes 442376 | tf_op jit(solution)/shard_map/ppermute | solution.py:26
  316.0 18.7 %collective-permute-start.22 = (bf16[24,3072]{1,0:T(8,128)(2,1)S(1)}, bf16[24,3072]{1,0:T(8,128)(2,1)S(1)}, u32[]{:S(2)}, u32[]{:S(2)}) collective-permute-start(bf16[24,3072]{1,0:T(8,128)(2,1)S(1)} %get-tuple-element.95), channel_id=1, source_target_pairs={{0,24},{1,25},{2,26},{3,27},{4,28},{5,29},{6,30},{7,31},{8,16},{9,... | collective-permute-start | bytes 442376 | tf_op jit(solution)/shard_map/ppermute | solution.py:26
  319.7 17.9 %collective-permute-start.21 = (bf16[24,3072]{1,0:T(8,128)(2,1)S(1)}, bf16[24,3072]{1,0:T(8,128)(2,1)S(1)}, u32[]{:S(2)}, u32[]{:S(2)}) collective-permute-start(bf16[24,3072]{1,0:T(8,128)(2,1)S(1)} %get-tuple-element.96), channel_id=1, source_target_pairs={{0,16},{1,17},{2,18},{3,19},{4,20},{5,21},{6,22},{7,23},{8,24},{9,... | collective-permute-start | bytes 442376 | tf_op jit(solution)/shard_map/ppermute | solution.py:26
  (26 other events, 167.4 us)
Sparse Core Ops, SparseCore 0:
  12.1 122.4 all-gather.1
where the time goes:
time: 346 us; the launch traced here: 345 us
  Pallas kernels  133 us (38%)
  waiting for transfers between devices  109 us (32%)
  starting transfers between devices  34.9 us (10%)
  local copies, waits for them, and re-layouts  21.4 us (6%)
  other arithmetic  20.3 us (6%)
  between operations  14.5 us (4%)
  matrix products  12.2 us (4%)
    ppermute x23, waiting for transfers between devices, swapped(): return lax.ppermute(value, AXIS, [(i, i ^ mask) for i in range(peers)])  87.5 us
    pallas_call x2, Pallas kernels, front(): pl.pallas_call(functools.partial(front_kernel, seq_len, windows, ln_rows)...  32.5 us
    ppermute x23, starting transfers between devices, swapped(): return lax.ppermute(value, AXIS, [(i, i ^ mask) for i in range(peers)])  22.3 us
    pallas_call x1, Pallas kernels, mlp_back(): pl.pallas_call(mlp_back_kernel, grid=(steps,), out_shape=[part] * 4 + [ja...  21.4 us
    pallas_call x1, Pallas kernels, attention_back(): pl.pallas_call(attention_back_kernel, out_shape=[jax.ShapeDtypeStruct((ro...  21.4 us
    all_gather x1, waiting for transfers between devices, local(): whole = lax.all_gather(shard, AXIS, axis=0, tiled=True)  16.7 us
    pallas_call x1, Pallas kernels, image_up(): pl.pallas_call(functools.partial(image_up_kernel, fold), grid=(FF // TILE...  14.1 us
    pallas_call x1, Pallas kernels, text_up(): pl.pallas_call(text_up_kernel, grid=(FF // TILE,), out_shape=[jax.ShapeDt...  13.8 us
  transfers between devices with their start and end apart: 27, of which 17 were waited for; matrix products, arithmetic and copies ran while one was open for 13% of the time, Pallas kernels for 39%

commit v1 on v0

--- a/solution.py
+++ b/solution.py
@@ -77,29 +77,22 @@
     return mul_bt(order, values).astype(bf16)
 
 
-def summed_pair(kept, got):
-    return (kept.astype(f32) + got.astype(f32)).astype(bf16)
-
-
-def scattered(keep_a, send_a, keep_b, send_b):
-    order_a, order_b, tail = stage_orders()
-    for k, (mask_a, mask_b) in enumerate(zip(order_a, order_b)):
-        got_a = swapped(send_a, mask_a)
-        got_b = swapped(send_b, mask_b)
-        half = keep_a.shape[0] // 2
-        if k + 1 < len(order_a):
-            send_a = summed_pair(keep_a[half:], got_a[half:])
-            send_b = summed_pair(keep_b[half:], got_b[half:])
-            keep_a = summed_pair(keep_a[:half], got_a[:half])
-            keep_b = summed_pair(keep_b[:half], got_b[:half])
-        else:
-            keep_a, keep_b = summed_pair(keep_a, got_a), summed_pair(keep_b, got_b)
-    both = jnp.concatenate([keep_a, keep_b], axis=1)
-    rows = both.shape[0] // 4
-    low, high = tail
-    total = both[:rows].astype(f32)
-    for k, mask in ((1, low), (2, high), (3, low | high)):
-        total = total + swapped(both[k * rows : (k + 1) * rows], mask).astype(f32)
+def hand_on(parts, stage):
+    order_a, order_b, _ = stage_orders()
+    keep_a, send_a, keep_b, send_b = parts
+    return keep_a, swapped(send_a, order_a[stage]), keep_b, swapped(send_b, order_b[stage])
+
+
+def hand_on_last(blocks):
+    low, high = stage_orders()[2]
+    own, *others = blocks
+    return own, [swapped(block, mask) for block, mask in zip(others, (low, high, low | high))]
+
+
+def sum_last(own, others):
+    total = own
+    for other in others:
+        total = total + other.astype(f32)
     return total
 
 
@@ -163,6 +156,68 @@
     scores = jnp.where(mask, scores, -1e30)
     raised = jnp.exp(scores - jnp.max(scores, axis=-1, keepdims=True))
     return raised * (1.0 / jnp.sum(raised, axis=-1, keepdims=True))
+
+
+def fold_kernel(keep_a, got_a, keep_b, got_b, *refs):
+    outs = refs[-4:]
+    half = outs[0].shape[0]
+    for k, (kept, got) in enumerate(((keep_a, got_a), (keep_b, got_b))):
+        for j in range(2):
+            at = slice(j * half, (j + 1) * half)
+            outs[2 * k + j][...] = (kept[at, :].astype(f32) + got[at, :].astype(f32)).astype(bf16)
+
+
+def fold(parts, after=()):
+    rows, cols = parts[0].shape
+    if rows % 32:
+        whole = [
+            (kept.astype(f32) + got.astype(f32)).astype(bf16)
+            for kept, got in (parts[:2], parts[2:])
+        ]
+        return [part for one in whole for part in (one[: rows // 2], one[rows // 2 :])]
+    tile = 512
+    return pl.pallas_call(
+        fold_kernel,
+        grid=(cols // tile,),
+        out_shape=[jax.ShapeDtypeStruct((rows // 2, cols), bf16)] * 4,
+        in_specs=[pl.BlockSpec((rows, tile), lambda i: (0, i))] * 4 + anywhere(after),
+        out_specs=[pl.BlockSpec((rows // 2, tile), lambda i: (0, i))] * 4,
+        compiler_params=params(),
+        cost_estimate=cost(2 * rows * cols, 12 * rows * cols),
+        name="fold",
+    )(*parts, *after)
+
+
+def fold_last_kernel(keep_a, got_a, keep_b, got_b, own_ref, *outs):
+    rows = own_ref.shape[0]
+    cols = keep_a.shape[1]
+    for k, (kept, got) in enumerate(((keep_a, got_a), (keep_b, got_b))):
+        total = kept[...].astype(f32) + got[...].astype(f32)
+        at = slice(k * cols, (k + 1) * cols)
+        own_ref[:, at] = total[:rows]
+        for j, out in enumerate(outs):
+            out[:, at] = total[(j + 1) * rows : (j + 2) * rows].astype(bf16)
+
+
+def fold_last(parts):
+    rows, cols = parts[0].shape
+    shape = (rows // 4, 2 * cols)
+    if rows % 32:
+        pairs = (parts[:2], parts[2:])
+        both = [kept.astype(f32) + got.astype(f32) for kept, got in pairs]
+        own, *others = jnp.split(jnp.concatenate(both, axis=1), 4)
+        return [own] + [other.astype(bf16) for other in others]
+    return pl.pallas_call(
+        fold_last_kernel,
+        out_shape=[jax.ShapeDtypeStruct(shape, f32)] + [jax.ShapeDtypeStruct(shape, bf16)] * 3,
+        compiler_params=params(),
+        cost_estimate=cost(2 * rows * cols, 12 * rows * cols),
+        name="fold_last",
+    )(*parts)
+
+
+def anywhere(after):
+    return [pl.BlockSpec(memory_space=pl.ANY)] * len(after)
 
 
 def pair_cols(part, pair):
@@ -456,8 +511,8 @@
 
 
 def loss_kernel(
-    pack_ref, image_ref, own_ref, unit_ref, inv_ref, loss_ref, row_ref, col_sum_ref, col_count_ref,
-    live_ref
+    pack_ref, image_ref, own_ref, unit_ref, inv_ref, loss_ref, row_ref, low_ref, col_sum_ref,
+    col_count_ref, live_ref
 ):
     image_all = image_ref[...]
     chunk = 256
@@ -474,23 +529,26 @@
     grad = grad_of_unit(
         own_ref[:, :D], own_ref[:, D:].astype(f32), image_all, col_sum, col_count, live_total
     )
-    row_ref[...] = inv_ref[:, :1] * turned(grad, unit_ref[...]) * (1.0 / TXT_LEN)
+    row = inv_ref[:, :1] * turned(grad, unit_ref[...]) * (1.0 / TXT_LEN)
+    row_ref[...] = row
+    low_ref[...] = row.astype(bf16)
 
 
 def loss_and_rows(pack, image_all, own_pack, unit, inverse):
     images, count = image_all.shape[0], own_pack.shape[0]
-    shapes = [(1, 128), (count, D), (1, images), (1, images), (1, 128)]
+    shapes = [(1, 128), (count, D), (count, D), (1, images), (1, images), (1, 128)]
+    kinds = [f32, f32, bf16, f32, f32, f32]
     return pl.pallas_call(
         loss_kernel,
-        out_shape=[jax.ShapeDtypeStruct(shape, f32) for shape in shapes],
+        out_shape=[jax.ShapeDtypeStruct(*item) for item in zip(shapes, kinds)],
         compiler_params=params(),
         cost_estimate=cost(2 * pack.shape[0] * images * D, 2 * pack.size, pack.shape[0] * images),
         name="loss_and_rows",
     )(pack, image_all, own_pack, unit, inverse)
 
 
-def down_kernel(pack_ref, image_ref, col_sum_ref, col_count_ref, live_ref, hid_ref, out_ref):
-    step = pl.program_id(0)
+def down_kernel(pack_ref, image_ref, col_sum_ref, col_count_ref, live_ref, hid_ref, *refs):
+    step, out_ref = pl.program_id(0), refs[-1]
     text_rows = pack_ref[:, :D]
     grad = grad_of_unit(
         text_rows, pack_ref[:, D:].astype(f32), image_ref[...], col_sum_ref[...],
@@ -508,7 +566,7 @@
         out_ref[...] += part
 
 
-def grad_of_down(pack, image_all, col_sum, col_count, live_total, hidden_cols):
+def grad_of_down(pack, image_all, col_sum, col_count, live_total, hidden_cols, after):
     images, chunk = image_all.shape[0], 256
     fixed = lambda shape: pl.BlockSpec(shape, lambda i: (0, 0))
     per = hidden_cols.shape[1]
@@ -520,12 +578,13 @@
             pl.BlockSpec((chunk, pack.shape[1]), lambda i: (i, 0)),
             fixed((images, D)), fixed((1, images)), fixed((1, images)), fixed((1, 128)),
             pl.BlockSpec((chunk, per), lambda i: (i, 0)),
-        ],
+        ]
+        + anywhere(after),
         out_specs=fixed((per, D)),
         compiler_params=params(),
         cost_estimate=cost(4 * pack.shape[0] * images * D, 2 * pack.size, pack.shape[0] * images),
         name="grad_of_down",
-    )(pack, image_all, col_sum, col_count, live_total, hidden_cols)
+    )(pack, image_all, col_sum, col_count, live_total, hidden_cols, *after)
 
 
 def mlp_back_kernel(
@@ -580,7 +639,7 @@
             out_ref[at, :] = row + norm_back(unit, scale, gain, grad)
 
 
-def mlp_back(grad_row, weight_down, slope, weight_up, lhs, middle, gain):
+def mlp_back(grad_row, grad_low, weight_down, slope, weight_up, lhs, middle, gain):
     rows, count = slope.shape[0], grad_row.shape[0]
     steps = FF // TILE
     fixed = lambda shape: pl.BlockSpec(shape, lambda i: (0, 0))
@@ -607,110 +666,135 @@
         compiler_params=params(),
         cost_estimate=cost(4 * rows * D * FF, 4 * D * FF + 2 * rows * FF + 2 * D * FF, rows * FF),
         name="mlp_back",
-    )(grad_row.astype(bf16), weight_down, slope, weight_up, lhs, middle, gain[None], grad_row)
-
-
-def attention_back_kernel(grad_ref, wo_ref, qkv_ref, low_ref, out_ref):
-    rows, chunk = grad_ref.shape[0], 128
+    )(grad_low, weight_down, slope, weight_up, lhs, middle, gain[None], grad_row)
+
+
+def attention_back_kernel(grad_ref, wo_ref, qkv_ref, *refs):
+    low_ref, out_ref = refs[-2:]
+    chunk = grad_ref.shape[0]
     one = same_sequence(chunk, 0, chunk, 0, TXT_LEN)
     mask = jnp.concatenate([one, one], axis=0)
-
-    @pl.loop(0, rows // chunk)
-    def _(step):
-        at = pl.ds(pl.multiple_of(step * chunk, chunk), chunk)
-        low_ref[at, :] = grad_ref[at, :].astype(bf16)
-
-    @pl.loop(0, rows // chunk)
-    def _(step):
-        at = pl.ds(pl.multiple_of(step * chunk, chunk), chunk)
-        grad_att = mul_bt(low_ref[at, :], wo_ref[...]).astype(bf16)
-        for pair in range(HEADS // 2):
-            queries = two_heads(qkv_ref[at, pair_cols(0, pair)] * bf16(HEAD ** (-0.5)))
-            keys = qkv_ref[at, pair_cols(1, pair)]
-            vals = qkv_ref[at, pair_cols(2, pair)]
-            grads = two_heads(grad_att[:, pair_cols(0, pair)])
-            probs = masked_softmax(mul_bt(queries, keys), mask)
-            grad_probs = mul_bt(grads, vals)
-            along = jnp.sum(grad_probs * probs, axis=-1, keepdims=True)
-            grad_scores = (probs * (grad_probs - along)).astype(bf16)
-            side = jnp.concatenate([grad_scores[:chunk], grad_scores[chunk:]], axis=1)
-            grad_q = mul(side, two_heads(keys)) * HEAD ** (-0.5)
-            grad_k = mul_at(grad_scores, queries)
-            grad_v = mul_at(probs.astype(bf16), grads)
-            out_ref[at, pair_cols(0, pair)] = grad_q.astype(bf16)
-            out_ref[at, pair_cols(1, pair)] = grad_k.astype(bf16)
-            out_ref[at, pair_cols(2, pair)] = grad_v.astype(bf16)
-
-
-def attention_back(grad_middle, weight_out, project):
-    rows = project.shape[0]
+    low = grad_ref[...].astype(bf16)
+    low_ref[...] = low
+    grad_att = mul_bt(low, wo_ref[...]).astype(bf16)
+    for pair in range(HEADS // 2):
+        queries = two_heads(qkv_ref[:, pair_cols(0, pair)] * bf16(HEAD ** (-0.5)))
+        keys = qkv_ref[:, pair_cols(1, pair)]
+        vals = qkv_ref[:, pair_cols(2, pair)]
+        grads = two_heads(grad_att[:, pair_cols(0, pair)])
+        probs = masked_softmax(mul_bt(queries, keys), mask)
+        grad_probs = mul_bt(grads, vals)
+        along = jnp.sum(grad_probs * probs, axis=-1, keepdims=True)
+        grad_scores = (probs * (grad_probs - along)).astype(bf16)
+        side = jnp.concatenate([grad_scores[:chunk], grad_scores[chunk:]], axis=1)
+        grad_q = mul(side, two_heads(keys)) * HEAD ** (-0.5)
+        grad_k = mul_at(grad_scores, queries)
+        grad_v = mul_at(probs.astype(bf16), grads)
+        out_ref[:, pair_cols(0, pair)] = grad_q.astype(bf16)
+        out_ref[:, pair_cols(1, pair)] = grad_k.astype(bf16)
+        out_ref[:, pair_cols(2, pair)] = grad_v.astype(bf16)
+
+
+def attention_back(grad_middle, weight_out, project, first, count, after=()):
+    chunk = 128
+    rows = count * chunk
     return pl.pallas_call(
         attention_back_kernel,
+        grid=(count,),
         out_shape=[
             jax.ShapeDtypeStruct((rows, D), bf16),
             jax.ShapeDtypeStruct((rows, 3 * D), bf16),
         ],
-        compiler_params=params(),
-        cost_estimate=cost(2 * rows * D * D, 16 * rows * D + 2 * D * D, rows * 128 * HEADS),
+        in_specs=[
+            pl.BlockSpec((chunk, D), lambda i: (i + first, 0)),
+            pl.BlockSpec((D, D), lambda i: (0, 0)),
+            pl.BlockSpec((chunk, 3 * D), lambda i: (i + first, 0)),
+        ]
+        + anywhere(after),
+        out_specs=[
+            pl.BlockSpec((chunk, D), lambda i: (i, 0)),
+            pl.BlockSpec((chunk, 3 * D), lambda i: (i, 0)),
+        ],
+        compiler_params=params(),
+        cost_estimate=cost(10 * rows * D * D, 16 * rows * D + 2 * D * D, rows * 128 * HEADS),
         name="attention_back",
-    )(grad_middle, weight_out, project)
-
-
-def weight_back_kernel(lhs_ref, proj_ref, low_ref, keep_a, send_a, keep_b, send_b):
+    )(grad_middle, weight_out, project, *after)
+
+
+def mul_rows(lhs, parts):
+    total, row = 0.0, 0
+    for part in parts:
+        total = total + mul(lhs[:, row : row + part.shape[0]], part[...])
+        row += part.shape[0]
+    return total
+
+
+def weight_back_kernel(count, lhs_ref, *refs):
     step = pl.program_id(0)
     half = D // 2
+    projs, lows = refs[:count], refs[count : 2 * count]
+    keep_a, send_a, keep_b, send_b = refs[-4:]
 
     @pl.when(step < 2)
     def _():
-        weight = mul(lhs_ref[0], proj_ref[...]).astype(bf16)
+        weight = mul_rows(lhs_ref[0], projs).astype(bf16)
         keep_a[...] = weight[:half]
         send_a[...] = weight[half:]
 
     @pl.when(step == 2)
     def _():
-        weight = mul(lhs_ref[0], proj_ref[...]).astype(bf16)
+        weight = mul_rows(lhs_ref[0], projs).astype(bf16)
         keep_b[...] = weight[:half]
         send_b[...] = weight[half:]
 
     @pl.when(step == 3)
     def _():
-        weight = mul(lhs_ref[0], low_ref[...]).astype(bf16)
+        weight = mul_rows(lhs_ref[0], lows).astype(bf16)
         keep_b[...] = weight[:half]
         send_b[...] = weight[half:]
 
 
-def weight_back(lhs, grad_proj, grad_low):
-    rows = grad_proj.shape[0]
+def weight_back(lhs, grad_projs, grad_lows, after=()):
+    rows = lhs.shape[2]
     first = pl.BlockSpec((D // 2, D), lambda i: (0, jnp.minimum(i, 1)))
     second = pl.BlockSpec((D // 2, D), lambda i: (0, jnp.maximum(i - 2, 0)))
     return pl.pallas_call(
-        weight_back_kernel,
+        functools.partial(weight_back_kernel, len(grad_projs)),
         grid=(4,),
         out_shape=[jax.ShapeDtypeStruct((D // 2, 2 * D), bf16)] * 4,
-        in_specs=[
-            pl.BlockSpec((1, D, rows), lambda i: (jnp.maximum(i - 1, 0), 0, 0)),
-            pl.BlockSpec((rows, D), lambda i: (0, jnp.minimum(i, 2))),
-            pl.BlockSpec((rows, D), lambda i: (0, 0)),
-        ],
+        in_specs=[pl.BlockSpec((1, D, rows), lambda i: (jnp.maximum(i - 1, 0), 0, 0))]
+        + [
+            pl.BlockSpec((part.shape[0], D), lambda i: (0, jnp.minimum(i, 2)))
+            for part in grad_projs
+        ]
+        + [pl.BlockSpec((part.shape[0], D), lambda i: (0, 0)) for part in grad_lows]
+        + anywhere(after),
         out_specs=[first, first, second, second],
         compiler_params=params(),
         cost_estimate=cost(8 * rows * D * D, 8 * rows * D + 14 * D * D),
         name="weight_back",
-    )(lhs, grad_proj, grad_low)
-
-
-def input_back_kernel(proj_ref, w_ref, x_ref, gain_ref, mid_ref, out_ref, gain_out, bias_out, acc):
+    )(lhs, *grad_projs, *grad_lows, *after)
+
+
+def input_back_kernel(count, *refs):
+    projs = refs[:count]
+    w_ref, x_ref, gain_ref, mid_ref = refs[count : count + 4]
+    out_ref, gain_out, bias_out, acc = refs[-4:]
     step = pl.program_id(0)
     rows, chunk = x_ref.shape[0], 128
-    added = mul_bt(proj_ref[...], w_ref[...])
-
-    @pl.when(step == 0)
-    def _():
-        acc[...] = added
-
-    @pl.when(step > 0)
-    def _():
-        acc[...] += added
+    row = 0
+    for part in projs:
+        at = slice(row, row + part.shape[0])
+        row += part.shape[0]
+        added = mul_bt(part[...], w_ref[...])
+
+        @pl.when(step == 0)
+        def _(at=at, added=added):
+            acc[at, :] = added
+
+        @pl.when(step > 0)
+        def _(at=at, added=added):
+            acc[at, :] += added
 
     @pl.when(step == pl.num_programs(0) - 1)
     def _():
@@ -728,25 +812,26 @@
             out_ref[at, :] = mid_ref[at, :] + norm_back(unit, scale, gain, grad)
 
 
-def input_back(grad_proj, weight, rows_in, gain, grad_middle):
+def input_back(grad_projs, weight, rows_in, gain, grad_middle, after=()):
     rows = rows_in.shape[0]
     fixed = lambda shape: pl.BlockSpec(shape, lambda i: (0, 0))
     line = jax.ShapeDtypeStruct((1, D), f32)
     return pl.pallas_call(
-        input_back_kernel,
+        functools.partial(input_back_kernel, len(grad_projs)),
         grid=(3,),
         out_shape=[jax.ShapeDtypeStruct((rows, D), f32), line, line],
-        in_specs=[
-            pl.BlockSpec((rows, D), lambda i: (0, i)),
+        in_specs=[pl.BlockSpec((part.shape[0], D), lambda i: (0, i)) for part in grad_projs]
+        + [
             pl.BlockSpec((D, D), lambda i: (0, i)),
             fixed((rows, D)), fixed((1, D)), fixed((rows, D)),
-        ],
+        ]
+        + anywhere(after),
         out_specs=[fixed((rows, D)), fixed((1, D)), fixed((1, D))],
         scratch_shapes=[pltpu.VMEM((rows, D), f32)],
         compiler_params=params(),
         cost_estimate=cost(6 * rows * D * D, 14 * rows * D + 6 * D * D),
         name="input_back",
-    )(grad_proj, weight, rows_in, gain[None], grad_middle)
+    )(*grad_projs, weight, rows_in, gain[None], grad_middle, *after)
 
 
 def local(
@@ -826,7 +911,7 @@
     )
 
     if small:
-        loss_value, grad_row, col_sum, col_count, live_total = loss_and_rows(
+        loss_value, grad_row, row_low, col_sum, col_count, live_total = loss_and_rows(
             text_pack, image_all, own_pack, text_unit, inverse
         )
         loss_value = loss_value[0, 0]
@@ -836,25 +921,36 @@
         loss_value = loss_from(sums)[0, 0]
         grad = grad_of_unit(text_low, pos, image_all, sums[0], sums[1], sums[4])
         grad_row = inverse[:, :1] * turned(grad, text_unit) * (1.0 / TXT_LEN)
-
-    *up_parts, grad_middle, gain_two, bias_two = mlp_back(
-        grad_row, txt_down, slope, txt_up, lhs_up, middle, txt_gain2
-    )
-    up_share = scattered(*up_parts)
+        row_low = grad_row.astype(bf16)
+
+    *up, grad_middle, gain_two, bias_two = mlp_back(
+        grad_row, row_low, txt_down, slope, txt_up, lhs_up, middle, txt_gain2
+    )
+    stages = len(order_a)
+    low_one, proj_one = attention_back(grad_middle, txt_out, project, 0, 2)
+    for stage in range(stages - 2):
+        up = fold(hand_on(up, stage), (proj_one,))
+    low_two, proj_two = attention_back(grad_middle, txt_out, project, 2, 3, up)
+    up = fold(hand_on(up, stages - 2), (proj_two,))
+    rest = weight_back(lhs_rest, (proj_one, proj_two), (low_one, low_two), up)
+    up = fold_last(hand_on(up, stages - 1))
+    caption_grad, gain_one, bias_one = input_back(
+        (proj_one, proj_two), txt_qkv, captions, txt_gain1, grad_middle, [*up, rest[0]]
+    )
+    for stage in range(stages - 2):
+        rest = fold(hand_on(rest, stage), (caption_grad,))
+    up_share = sum_last(*hand_on_last(up))
     if small:
-        grad_down = grad_of_down(text_pack, image_all, col_sum, col_count, live_total, hidden_cols)
+        grad_down = grad_of_down(
+            text_pack, image_all, col_sum, col_count, live_total, hidden_cols, rest
+        )
+        rest = fold(hand_on(rest, stages - 2), (grad_down,))
     else:
         grad_down = lax.psum_scatter(
-            mul_at(hidden_sum.astype(bf16), grad_row.astype(bf16)),
-            AXIS,
-            scatter_dimension=0,
-            tiled=True,
+            mul_at(hidden_sum.astype(bf16), row_low), AXIS, scatter_dimension=0, tiled=True
         )
-    grad_low, grad_proj = attention_back(grad_middle, txt_out, project)
-    rest_share = scattered(*weight_back(lhs_rest, grad_proj, grad_low))
-    caption_grad, gain_one, bias_one = input_back(
-        grad_proj, txt_qkv, captions, txt_gain1, grad_middle
-    )
+        rest = fold(hand_on(rest, stages - 2))
+    rest_share = sum_last(*hand_on_last(fold_last(hand_on(rest, stages - 1))))
     norms = jnp.concatenate([gain_one, bias_one, gain_two, bias_two], axis=0)
     norms = jnp.sum(spread(norms[None]), axis=0).reshape(4, D)
     return (

time: 346 us -> 345 us (level)
  Pallas kernels: 133 us -> 155 us
  waiting for transfers between devices: 109 us -> 96.7 us
  other arithmetic: 20.3 us -> 9.66 us
  local copies, waits for them, and re-layouts: 21.4 us -> 24.9 us
    pallas_call x4 -> x11, Pallas kernels: 43.5 us -> 65.3 us  [the longest x2 21.8 us: attention_back(): pl.pallas_call(attention_back_kernel, grid=(count,), out_shape=[jax.Shape...]
    ppermute x23, waiting for transfers between devices: 87.5 us -> 79 us  [swapped(): return lax.ppermute(value, AXIS, [(i, i ^ mask) for i in range(peers)])]
    convert_element_type x13 -> x0, other arithmetic: 7.36 us -> none  [the longest x12 5.83 us: summed_pair(): return (kept.astype(f32) + got.astype(f32)).astype(bf16)]
    unnamed x47 -> x77, local copies, waits for them, and re-layouts: 2.1 us -> 7.57 us
  transfers between devices with their start and end apart: 27 -> 27, of which waited for: 17 -> 14; matrix products, arithmetic and copies ran while one was open for 13% -> 9% of each run, Pallas kernels for 39% -> 33%
where the time goes in v1:
time: 345 us; the launch traced here: 344 us
  Pallas kernels  155 us (45%)
  waiting for transfers between devices  96.7 us (28%)
  starting transfers between devices  33.8 us (10%)
  local copies, waits for them, and re-layouts  24.9 us (7%)
  between operations  14.6 us (4%)
  other arithmetic  9.66 us (3%)
  matrix products  9.12 us (3%)
    ppermute x23, waiting for transfers between devices, swapped(): return lax.ppermute(value, AXIS, [(i, i ^ mask) for i in range(peers)])  79 us
    pallas_call x2, Pallas kernels, front(): pl.pallas_call(functools.partial(front_kernel, seq_len, windows, ln_rows)...  32.4 us
    ppermute x23, starting transfers between devices, swapped(): return lax.ppermute(value, AXIS, [(i, i ^ mask) for i in range(peers)])  25.3 us
    pallas_call x2, Pallas kernels, attention_back(): pl.pallas_call(attention_back_kernel, grid=(count,), out_shape=[jax.Shape...  21.8 us
    pallas_call x1, Pallas kernels, mlp_back(): pl.pallas_call(mlp_back_kernel, grid=(steps,), out_shape=[part] * 4 + [ja...  21.5 us
    pallas_call x4, Pallas kernels, fold(): pl.pallas_call(fold_kernel, grid=(cols // tile,), out_shape=[jax.ShapeDty...  16.2 us
    pallas_call x1, Pallas kernels, image_up(): pl.pallas_call(functools.partial(image_up_kernel, fold), grid=(FF // TILE...  14.1 us
    pallas_call x1, Pallas kernels, text_up(): pl.pallas_call(text_up_kernel, grid=(FF // TILE,), out_shape=[jax.ShapeDt...  13.7 us
  transfers between devices with their start and end apart: 27, of which 14 were waited for; matrix products, arithmetic and copies ran while one was open for 9% of the time, Pallas kernels for 33%

profile of v1, /device:TPU:0, one launch (start us, length us, event | category | flops | bytes accessed | tf_op | source)
XLA Modules:
  0.0 343.6 jit_solution(8537396555093109100)
XLA Ops:
  15.1 18.7 %front.2 = (bf16[640,768]{1,0:T(8,128)(2,1)}, bf16[640,2304]{1,0:T(8,128)(2,1)}, bf16[640,768]{1,0:T(8,128)(2,1)}, f32[640,768]{1,0:T(8,128)}, bf16[640,768]{1,0:T(8,128)(2,1)}, /*index=5*/f32[40,768]{1,0:T(8,128)}) custom-call(bf16[640,768]{1,0:T(8,128)(2,1)} %refs_3_.1, f32[1,768]{1,0:T(1,128)} %broadcast_in_dim.22.g1_ref.refs_4_, ...), custom_call_target="tpu_custom_call" | custom-call | flops 3019898880 | bytes 11599872 | tf_op jit(solution)/shard_map/front/pallas_call | solution.py:318
  33.7 13.7 %text_up.1 = (bf16[640,3072]{1,0:T(8,128)(2,1)}, f32[40,3072]{1,0:T(8,128)}, f32[40,768]{1,0:T(8,128)}, f32[40,128]{1,0:T(8,128)}) custom-call(bf16[640,768]{1,0:T(8,128)(2,1)} %get-tuple-element.70.h2_ref, bf16[768,3072]{1,0:T(8,128)(2,1)} %wu_ref.3, bf16[3072,768]{1,0:T(8,128)(2,1)} %wd_ref.3, f32[40,768]{1,0:T(8,128)} %get-tuple-element.71.sum_ref), custom_call_target="tpu_custom_call" | custom-call | flops 3019898880 | bytes 13369344 | tf_op jit(solution)/shard_map/text_up/pallas_call | solution.py:387
  49.9 4.1 %collective-permute-start = (bf16[1,40,1024]{2,1,0:T(8,128)(2,1)S(1)}, bf16[1,40,1024]{2,1,0:T(8,128)(2,1)S(1)}, u32[]{:S(2)}, u32[]{:S(2)}) collective-permute-start(bf16[1,40,1024]{2,1,0:T(8,128)(2,1)S(1)} %get-tuple-element.145), channel_id=1, source_target_pairs={{0,16},{1,17},{2,18},{3,19},{4,20},{5,21},{6,22},{7,23},{8,24},{9,... | collective-permute-start | bytes 245768 | tf_op jit(solution)/shard_map/ppermute | solution.py:26
  54.0 8.6 %collective-permute-done = bf16[1,40,1024]{2,1,0:T(8,128)(2,1)S(1)} collective-permute-done((bf16[1,40,1024]{2,1,0:T(8,128)(2,1)S(1)}, bf16[1,40,1024]{2,1,0:T(8,128)(2,1)S(1)}, u32[]{:S(2)}, u32[]{:S(2)}) %collective-permute-start) | collective-permute-done | bytes 81952 | tf_op jit(solution)/shard_map/ppermute | solution.py:26
  62.7 9.3 %collective-permute-done.1 = bf16[2,40,1024]{2,1,0:T(8,128)(2,1)S(1)} collective-permute-done((bf16[2,40,1024]{2,1,0:T(8,128)(2,1)S(1)}, bf16[2,40,1024]{2,1,0:T(8,128)(2,1)S(1)}, u32[]{:S(2)}, u32[]{:S(2)}) %collective-permute-start.1) | collective-permute-done | bytes 163872 | tf_op jit(solution)/shard_map/ppermute | solution.py:26
  73.6 14.3 %collective-permute-done.2 = bf16[4,40,1024]{2,1,0:T(8,128)(2,1)S(1)} collective-permute-done((bf16[4,40,1024]{2,1,0:T(8,128)(2,1)S(1)}, bf16[4,40,1024]{2,1,0:T(8,128)(2,1)S(1)}, u32[]{:S(2)}, u32[]{:S(2)}) %collective-permute-start.2) | collective-permute-done | bytes 327712 | tf_op jit(solution)/shard_map/ppermute | solution.py:26
  88.7 27.0 %collective-permute-done.3 = bf16[8,40,1024]{2,1,0:T(8,128)(2,1)S(1)} collective-permute-done((bf16[8,40,1024]{2,1,0:T(8,128)(2,1)S(1)}, bf16[8,40,1024]{2,1,0:T(8,128)(2,1)S(1)}, u32[]{:S(2)}, u32[]{:S(2)}) %collective-permute-start.3) | collective-permute-done | bytes 655392 | tf_op jit(solution)/shard_map/ppermute | solution.py:26
  121.3 13.3 %all-gather.2.cloned.1.call-done.wqkv_ref.wo_ref.wu_ref.wd_ref = bf16[768,9216]{1,0:T(8,128)(2,1)} async-done(((bf16[24,9216]{1,0:T(8,128)(2,1)}), bf16[768,9216]{1,0:T(8,128)(2,1)}) %all-gather.2.cloned.1.call-update) | async-done | bytes 14155792 | tf_op jit(solution)/shard_map/all_gather | solution.py:875
  134.6 13.7 %front.3 = (bf16[400,768]{1,0:T(8,128)(2,1)}, bf16[400,2304]{1,0:T(8,128)(2,1)}, bf16[400,768]{1,0:T(8,128)(2,1)}, f32[400,768]{1,0:T(8,128)}, bf16[400,768]{1,0:T(8,128)(2,1)}, /*index=5*/f32[8,768]{1,0:T(8,128)}) custom-call(bf16[400,768]{1,0:T(8,128)(2,1)} %x_ref.3, bf16[1,768]{1,0:T(2,128)(2,1)} %broadcast_in_dim.54.g1_ref, ...), custom_call_target="tpu_custom_call" | custom-call | flops 1887436800 | bytes 9019392 | tf_op jit(solution)/shard_map/front/pallas_call | solution.py:318
  148.3 14.1 %image_up.1 = bf16[8,768]{1,0:T(8,128)(2,1)} custom-call(bf16[400,768]{1,0:T(8,128)(2,1)} %get-tuple-element.73.h2_ref, bf16[768,9216]{1,0:T(8,128)(2,1)} %all-gather.2.cloned.1.call-done.wqkv_ref.wo_ref.wu_ref.wd_ref, bf16[768,9216]{1,0:T(8,128)(2,1)} %all-gather.2.cloned.1.call-done.wqkv_ref.wo_ref.wu_ref.wd_ref, f32[8,768]{1,0:T(8,128)} %get-tuple-element.74.sum_ref), custom_call_target="tpu_custom_call" | custom-call | flops 1887436800 | bytes 9437184 | tf_op jit(solution)/shard_map/image_up/pallas_call | solution.py:452
  175.5 4.3 %all-to-all-done = bf16[32,8,768]{2,1,0:T(8,128)(2,1)S(1)} async-done(((bf16[32,8,768]{2,1,0:T(8,128)(2,1)}), bf16[32,8,768]{2,1,0:T(8,128)(2,1)S(1)}, u32[]{:S(2)}, u32[]{:S(2)}) %all-to-all-start) | async-done | bytes 393248 | tf_op jit(solution)/shard_map/all_to_all | solution.py:49
  180.6 4.0 %loss_and_rows.1 = (f32[1,128]{1,0:T(1,128)}, f32[40,768]{1,0:T(8,128)}, bf16[40,768]{1,0:T(8,128)(2,1)}, f32[1,256]{1,0:T(1,128)}, f32[1,256]{1,0:T(1,128)}, /*index=5*/f32[1,128]{1,0:T(1,128)}) custom-call(bf16[1280,1024]{1,0:T(8,128)(2,1)} %bitcast.68, bf16[256,768]{1,0:T(8,128)(2,1)} %bitcast.71, bf16[40,1024]{1,0:T(8,128)(2,1)} %get-tuple-element.144.own_ref, ...), custom_call_target="tpu_custom_call" | custom-call | flops 503316480 | bytes 2621440 | tf_op jit(solution)/shard_map/loss_and_rows/pallas_call | solution.py:541
  184.6 21.5 %mlp_back.1 = (bf16[384,1536]{1,0:T(8,128)(2,1)}, bf16[384,1536]{1,0:T(8,128)(2,1)}, bf16[384,1536]{1,0:T(8,128)(2,1)}, bf16[384,1536]{1,0:T(8,128)(2,1)}, f32[6...) custom-call(bf16[40,768]{1,0:T(8,128)(2,1)} %get-tuple-element.77.low_ref, bf16[3072,768]{1,0:T(8,128)(2,1)} %wd_ref.3, ...), custom_call_target="tpu_custom_call" | custom-call | flops 6039797760 | bytes 18087936 | tf_op jit(solution)/shard_map/mlp_back/pallas_call | solution.py:650
  209.1 9.2 %attention_back.2 = (bf16[256,768]{1,0:T(8,128)(2,1)}, bf16[256,2304]{1,0:T(8,128)(2,1)}) custom-call(f32[640,768]{1,0:T(8,128)} %get-tuple-element.81.grad_ref.refs_5_, bf16[768,768]{1,0:T(8,128)(2,1)} %wo_ref.5, bf16[640,2304]{1,0:T(8,128)(2,1)} %get-tuple-element.82.qkv_ref), custom_call_target="tpu_custom_call" | custom-call | flops 1509949440 | bytes 4325376 | tf_op jit(solution)/shard_map/attention_back/pallas_call | solution.py:701
  219.8 4.6 %fold.4 = (bf16[192,1536]{1,0:T(8,128)(2,1)}, bf16[192,1536]{1,0:T(8,128)(2,1)}, bf16[192,1536]{1,0:T(8,128)(2,1)}, bf16[192,1536]{1,0:T(8,128)(2,1)}) custom-call(bf16[384,1536]{1,0:T(8,128)(2,1)} %get-tuple-element.84.keep_a, bf16[384,1536]{1,0:T(8,128)(2,1)} %copy-done.6, bf16[384,1536]{1,0:T(8,128)(2,1)} %get-tuple-element.86.keep_b, ...), custom_call_target="tpu_custom_call" | custom-call | flops 1179648 | bytes 7077888 | tf_op jit(solution)/shard_map/fold/pallas_call | solution.py:179
  229.5 12.6 %attention_back.3 = (bf16[384,768]{1,0:T(8,128)(2,1)}, bf16[384,2304]{1,0:T(8,128)(2,1)}) custom-call(f32[640,768]{1,0:T(8,128)} %get-tuple-element.81.grad_ref.refs_5_, bf16[768,768]{1,0:T(8,128)(2,1)} %wo_ref.5, bf16[640,2304]{1,0:T(8,128)(2,1)} %get-tuple-element.82.qkv_ref, bf16[192,1536]{1,0:T(8,128)(2,1)} %get-tuple-element.88.refs_0_.keep_a, ...), custom_call_target="tpu_custom_call" | custom-call | flops 2264924160 | bytes 5898240 | tf_op jit(solution)/shard_map/attention_back/pallas_call | solution.py:701
  243.1 3.5 %fold.5 = (bf16[96,1536]{1,0:T(8,128)(2,1)}, bf16[96,1536]{1,0:T(8,128)(2,1)}, bf16[96,1536]{1,0:T(8,128)(2,1)}, bf16[96,1536]{1,0:T(8,128)(2,1)}) custom-call(bf16[192,1536]{1,0:T(8,128)(2,1)} %get-tuple-element.88.refs_0_.keep_a, bf16[192,1536]{1,0:T(8,128)(2,1)} %copy-done.10, bf16[192,1536]{1,0:T(8,128)(2,1)} %get-tuple-element.90.refs_2_.keep_b, ...), custom_call_target="tpu_custom_call" | custom-call | flops 589824 | bytes 3538944 | tf_op jit(solution)/shard_map/fold/pallas_call | solution.py:179
  246.6 8.7 %weight_back.1 = (bf16[384,1536]{1,0:T(8,128)(2,1)}, bf16[384,1536]{1,0:T(8,128)(2,1)}, bf16[384,1536]{1,0:T(8,128)(2,1)}, bf16[384,1536]{1,0:T(8,128)(2,1)}) custom-call(bf16[3,768,640]{2,1,0:T(8,128)(2,1)} %pad_maximum_fusion.lhs_ref, bf16[256,2304]{1,0:T(8,128)(2,1)} %get-tuple-element.83.refs_0_, bf16[384,2304]{1,0:T(8,128)(2,1)} %get-tuple-element.92.refs_0_.refs_1_, ...), custom_call_target="tpu_custom_call" | custom-call | flops 3019898880 | bytes 12189696 | tf_op jit(solution)/shard_map/weight_back/pallas_call | solution.py:761
  268.3 10.4 %input_back.1 = (f32[640,768]{1,0:T(8,128)}, f32[1,768]{1,0:T(1,128)}, f32[1,768]{1,0:T(1,128)}) custom-call(bf16[256,2304]{1,0:T(8,128)(2,1)} %get-tuple-element.83.refs_0_, bf16[384,2304]{1,0:T(8,128)(2,1)} %get-tuple-element.92.refs_0_.refs_1_, bf16[768,2304]{1,0:T(8,128)(2,1)} %refs_2_.1, bf16[640,768]{1,0:T(8,128)(2,1)} %refs_3_.1, ...), custom_call_target="tpu_custom_call" | custom-call | flops 2264924160 | bytes 10420224 | tf_op jit(solution)/shard_map/input_back/pallas_call | solution.py:819
  280.1 4.6 %fold.6 = (bf16[192,1536]{1,0:T(8,128)(2,1)}, bf16[192,1536]{1,0:T(8,128)(2,1)}, bf16[192,1536]{1,0:T(8,128)(2,1)}, bf16[192,1536]{1,0:T(8,128)(2,1)}) custom-call(bf16[384,1536]{1,0:T(8,128)(2,1)} %get-tuple-element.105.refs_10_.keep_a, bf16[384,1536]{1,0:T(8,128)(2,1)} %copy-done.3, bf16[384,1536]{1,0:T(8,128)(2,1)} %get-tuple-element.112.keep_b, ...), custom_call_target="tpu_custom_call" | custom-call | flops 1179648 | bytes 7077888 | tf_op jit(solution)/shard_map/fold/pallas_call | solution.py:179
  291.3 7.9 %grad_of_down.1.refs_0_ = f32[96,768]{1,0:T(8,128)} custom-call(bf16[1280,1024]{1,0:T(8,128)(2,1)} %bitcast.69, bf16[256,768]{1,0:T(8,128)(2,1)} %bitcast.72, f32[1,256]{1,0:T(1,128)} %get-tuple-element.118.col_sum_ref, f32[1,256]{1,0:T(1,128)} %get-tuple-element.119.col_count_ref, f32[1,128]{1,0:T(1,128)} %get-tuple-element.120.live_ref, ...), custom_call_target="tpu_custom_call" | custom-call | flops 1006632960 | bytes 2621440 | tf_op jit(solution)/shard_map/grad_of_down/pallas_call | solution.py:573
  299.2 3.6 %collective-permute-done.13.got_a = bf16[192,1536]{1,0:T(8,128)(2,1)S(1)} collective-permute-done((bf16[192,1536]{1,0:T(8,128)(2,1)}, bf16[192,1536]{1,0:T(8,128)(2,1)S(1)}, u32[]{:S(2)}, u32[]{:S(2)}) %collective-permute-start.13) | collective-permute-done | bytes 589856 | tf_op jit(solution)/shard_map/ppermute | solution.py:26
  304.4 3.5 %fold.7 = (bf16[96,1536]{1,0:T(8,128)(2,1)}, bf16[96,1536]{1,0:T(8,128)(2,1)}, bf16[96,1536]{1,0:T(8,128)(2,1)}, bf16[96,1536]{1,0:T(8,128)(2,1)}) custom-call(bf16[192,1536]{1,0:T(8,128)(2,1)} %get-tuple-element.114.refs_0_.keep_a, bf16[192,1536]{1,0:T(8,128)(2,1)} %copy-done.8, bf16[192,1536]{1,0:T(8,128)(2,1)} %get-tuple-element.116.refs_2_.keep_b, ...), custom_call_target="tpu_custom_call" | custom-call | flops 589824 | bytes 3538944 | tf_op jit(solution)/shard_map/fold/pallas_call | solution.py:179
  326.7 8.6 %collective-permute-done.18 = bf16[24,3072]{1,0:T(8,128)(2,1)S(1)} collective-permute-done((bf16[24,3072]{1,0:T(8,128)(2,1)}, bf16[24,3072]{1,0:T(8,128)(2,1)S(1)}, u32[]{:S(2)}, u32[]{:S(2)}) %collective-permute-start.18) | collective-permute-done | bytes 147488 | tf_op jit(solution)/shard_map/ppermute | solution.py:26
  (184 shorter events, 85.3 us)
Async XLA Ops:
  7.2 127.4 %all-gather.2.cloned.1.call-start = ((), (), s32[]{:S(2)}) async-start(), calls=%async_computation.3 | async-start | bytes 14598144 | tf_op jit(solution)/shard_map/all_gather | solution.py:875
  49.9 12.7 %collective-permute-start = (bf16[1,40,1024]{2,1,0:T(8,128)(2,1)S(1)}, bf16[1,40,1024]{2,1,0:T(8,128)(2,1)S(1)}, u32[]{:S(2)}, u32[]{:S(2)}) collective-permute-start(bf16[1,40,1024]{2,1,0:T(8,128)(2,1)S(1)} %get-tuple-element.145), channel_id=1, source_target_pairs={{0,16},{1,17},{2,18},{3,19},{4,20},{5,21},{6,22},{7,23},{8,24},{9,... | collective-permute-start | bytes 245768 | tf_op jit(solution)/shard_map/ppermute | solution.py:26
  62.6 9.4 %collective-permute-start.1 = (bf16[2,40,1024]{2,1,0:T(8,128)(2,1)S(1)}, bf16[2,40,1024]{2,1,0:T(8,128)(2,1)S(1)}, u32[]{:S(2)}, u32[]{:S(2)}) collective-permute-start(bf16[2,40,1024]{2,1,0:T(8,128)(2,1)S(1)} %maximum_bitcast_fusion), channel_id=1, source_target_pairs={{0,8},{1,9},{2,10},{3,11},{4,12},{5,13},{6,14},{7,15},{8,0},{9,1},... | collective-permute-start | bytes 491528 | tf_op jit(solution)/shard_map/ppermute | solution.py:26
  72.1 15.8 %collective-permute-start.2 = (bf16[4,40,1024]{2,1,0:T(8,128)(2,1)S(1)}, bf16[4,40,1024]{2,1,0:T(8,128)(2,1)S(1)}, u32[]{:S(2)}, u32[]{:S(2)}) collective-permute-start(bf16[4,40,1024]{2,1,0:T(8,128)(2,1)S(1)} %bitcast.75), channel_id=1, source_target_pairs={{0,4},{1,5},{2,6},{3,7},{4,0},{5,1},{6,2},{7,3},{8,12},{9,13},{10,... | collective-permute-start | bytes 983048 | tf_op jit(solution)/shard_map/ppermute | solution.py:26
  88.1 27.7 %collective-permute-start.3 = (bf16[8,40,1024]{2,1,0:T(8,128)(2,1)S(1)}, bf16[8,40,1024]{2,1,0:T(8,128)(2,1)S(1)}, u32[]{:S(2)}, u32[]{:S(2)}) collective-permute-start(bf16[8,40,1024]{2,1,0:T(8,128)(2,1)S(1)} %bitcast.73), channel_id=1, source_target_pairs={{0,2},{1,3},{2,0},{3,1},{4,6},{5,7},{6,4},{7,5},{8,10},{9,11},{10,... | collective-permute-start | bytes 1966088 | tf_op jit(solution)/shard_map/ppermute | solution.py:26
  116.2 57.0 %collective-permute-start.4 = (bf16[16,40,1024]{2,1,0:T(8,128)(2,1)S(1)}, bf16[16,40,1024]{2,1,0:T(8,128)(2,1)S(1)}, u32[]{:S(2)}, u32[]{:S(2)}) collective-permute-start(bf16[16,40,1024]{2,1,0:T(8,128)(2,1)S(1)} %bitcast.70), channel_id=1, source_target_pairs={{0,1},{1,0},{2,3},{3,2},{4,5},{5,4},{6,7},{7,6},{8,9},{9,8},{10,11... | collective-permute-start | bytes 3932168 | tf_op jit(solution)/shard_map/ppermute | solution.py:26
  163.8 16.0 %all-to-all-start = ((bf16[32,8,768]{2,1,0:T(8,128)(2,1)}), bf16[32,8,768]{2,1,0:T(8,128)(2,1)S(1)}, u32[]{:S(2)}, u32[]{:S(2)}) async-start(bf16[32,8,768]{2,1,0:T(8,128)(2,1)} %broadcast_in_dim.58), calls=%async_computation | async-start | bytes 786432 | tf_op jit(solution)/shard_map/all_to_all | solution.py:49
  206.1 12.2 %collective-permute-start.5 = (bf16[384,1536]{1,0:T(8,128)(2,1)}, bf16[384,1536]{1,0:T(8,128)(2,1)S(1)}, u32[]{:S(2)}, u32[]{:S(2)}) collective-permute-start(bf16[384,1536]{1,0:T(8,128)(2,1)} %get-tuple-element.85), channel_id=1, source_target_pairs={{0,1},{1,0},{2,3},{3,2},{4,5},{5,4},{6,7},{7,6},{8,9},{9,8},{10,11... | collective-permute-start | bytes 3538952 | tf_op jit(solution)/shard_map/ppermute | solution.py:26
  206.2 12.1 %collective-permute-start.6 = (bf16[384,1536]{1,0:T(8,128)(2,1)}, bf16[384,1536]{1,0:T(8,128)(2,1)S(1)}, u32[]{:S(2)}, u32[]{:S(2)}) collective-permute-start(bf16[384,1536]{1,0:T(8,128)(2,1)} %get-tuple-element.87), channel_id=1, source_target_pairs={{0,1},{1,0},{2,3},{3,2},{4,5},{5,4},{6,7},{7,6},{8,9},{9,8},{10,11... | collective-permute-start | bytes 3538952 | tf_op jit(solution)/shard_map/ppermute | solution.py:26
  224.4 17.7 %collective-permute-start.7 = (bf16[192,1536]{1,0:T(8,128)(2,1)}, bf16[192,1536]{1,0:T(8,128)(2,1)S(1)}, u32[]{:S(2)}, u32[]{:S(2)}) collective-permute-start(bf16[192,1536]{1,0:T(8,128)(2,1)} %get-tuple-element.89.refs_1_), channel_id=1, source_target_pairs={{0,2},{1,3},{2,0},{3,1},{4,6},{5,7},{6,4},{7,5},{8,10},{9,11},{10,... | collective-permute-start | bytes 1769480 | tf_op jit(solution)/shard_map/ppermute | solution.py:26
  224.9 17.2 %collective-permute-start.8 = (bf16[192,1536]{1,0:T(8,128)(2,1)}, bf16[192,1536]{1,0:T(8,128)(2,1)S(1)}, u32[]{:S(2)}, u32[]{:S(2)}) collective-permute-start(bf16[192,1536]{1,0:T(8,128)(2,1)} %get-tuple-element.91.refs_3_), channel_id=1, source_target_pairs={{0,4},{1,5},{2,6},{3,7},{4,0},{5,1},{6,2},{7,3},{8,12},{9,13},{10,... | collective-permute-start | bytes 1769480 | tf_op jit(solution)/shard_map/ppermute | solution.py:26
  255.3 23.3 %collective-permute-start.11 = (bf16[384,1536]{1,0:T(8,128)(2,1)}, bf16[384,1536]{1,0:T(8,128)(2,1)S(1)}, u32[]{:S(2)}, u32[]{:S(2)}) collective-permute-start(bf16[384,1536]{1,0:T(8,128)(2,1)} %get-tuple-element.111), channel_id=1, source_target_pairs={{0,1},{1,0},{2,3},{3,2},{4,5},{5,4},{6,7},{7,6},{8,9},{9,8},{10,11... | collective-permute-start | bytes 3538952 | tf_op jit(solution)/shard_map/ppermute | solution.py:26
  255.3 23.3 %collective-permute-start.12 = (bf16[384,1536]{1,0:T(8,128)(2,1)}, bf16[384,1536]{1,0:T(8,128)(2,1)S(1)}, u32[]{:S(2)}, u32[]{:S(2)}) collective-permute-start(bf16[384,1536]{1,0:T(8,128)(2,1)} %get-tuple-element.113), channel_id=1, source_target_pairs={{0,1},{1,0},{2,3},{3,2},{4,5},{5,4},{6,7},{7,6},{8,9},{9,8},{10,11... | collective-permute-start | bytes 3538952 | tf_op jit(solution)/shard_map/ppermute | solution.py:26
  255.9 9.5 %collective-permute-start.9 = (bf16[96,1536]{1,0:T(8,128)(2,1)}, bf16[96,1536]{1,0:T(8,128)(2,1)S(1)}, u32[]{:S(2)}, u32[]{:S(2)}) collective-permute-start(bf16[96,1536]{1,0:T(8,128)(2,1)} %get-tuple-element.94.refs_5_), channel_id=1, source_target_pairs={{0,4},{1,5},{2,6},{3,7},{4,0},{5,1},{6,2},{7,3},{8,12},{9,13},{10,... | collective-permute-start | bytes 884744 | tf_op jit(solution)/shard_map/ppermute | solution.py:26
  256.6 9.5 %collective-permute-start.10 = (bf16[96,1536]{1,0:T(8,128)(2,1)}, bf16[96,1536]{1,0:T(8,128)(2,1)}, u32[]{:S(2)}, u32[]{:S(2)}) collective-permute-start(bf16[96,1536]{1,0:T(8,128)(2,1)} %get-tuple-element.96.refs_7_), channel_id=1, source_target_pairs={{0,2},{1,3},{2,0},{3,1},{4,6},{5,7},{6,4},{7,5},{8,10},{9,11},{10,... | collective-permute-start | bytes 884744 | tf_op jit(solution)/shard_map/ppermute | solution.py:26
  259.4 28.2 %all-to-all-start.2 = ((bf16[40,32,96]{2,0,1:T(8,128)(2,1)}), bf16[40,32,96]{2,0,1:T(8,128)(2,1)S(1)}, u32[]{:S(2)}, u32[]{:S(2)}) async-start(bf16[40,32,96]{2,0,1:T(8,128)(2,1)} %copy.57), calls=%async_computation.2 | async-start | bytes 655360 | tf_op jit(solution)/shard_map/all_to_all | solution.py:895
  284.6 18.1 %collective-permute-start.13 = (bf16[192,1536]{1,0:T(8,128)(2,1)}, bf16[192,1536]{1,0:T(8,128)(2,1)S(1)}, u32[]{:S(2)}, u32[]{:S(2)}) collective-permute-start(bf16[192,1536]{1,0:T(8,128)(2,1)} %get-tuple-element.115.refs_1_), channel_id=1, source_target_pairs={{0,2},{1,3},{2,0},{3,1},{4,6},{5,7},{6,4},{7,5},{8,10},{9,11},{10,... | collective-permute-start | bytes 1769480 | tf_op jit(solution)/shard_map/ppermute | solution.py:26
  287.3 16.2 %collective-permute-start.14 = (bf16[192,1536]{1,0:T(8,128)(2,1)}, bf16[192,1536]{1,0:T(8,128)(2,1)S(1)}, u32[]{:S(2)}, u32[]{:S(2)}) collective-permute-start(bf16[192,1536]{1,0:T(8,128)(2,1)} %get-tuple-element.117.refs_3_), channel_id=1, source_target_pairs={{0,4},{1,5},{2,6},{3,7},{4,0},{5,1},{6,2},{7,3},{8,12},{9,13},{10,... | collective-permute-start | bytes 1769480 | tf_op jit(solution)/shard_map/ppermute | solution.py:26
  288.4 36.9 %all-to-all-start.1 = ((f32[32,1,4,768]{3,2,1,0:T(4,128)}), f32[32,1,4,768]{3,2,1,0:T(4,128)S(1)}, u32[]{:S(2)}, u32[]{:S(2)}) async-start(f32[32,1,4,768]{3,2,1,0:T(4,128)} %broadcast_in_dim.59), calls=%async_computation.1 | async-start | bytes 786432 | tf_op jit(solution)/shard_map/all_to_all | solution.py:49
  310.0 11.8 %collective-permute-start.20 = (bf16[24,3072]{1,0:T(8,128)(2,1)S(1)}, bf16[24,3072]{1,0:T(8,128)(2,1)S(1)}, u32[]{:S(2)}, u32[]{:S(2)}) collective-permute-start(bf16[24,3072]{1,0:T(8,128)(2,1)S(1)} %copy-done.19), channel_id=1, source_target_pairs={{0,8},{1,9},{2,10},{3,11},{4,12},{5,13},{6,14},{7,15},{8,0},{9,1},... | collective-permute-start | bytes 442376 | tf_op jit(solution)/shard_map/ppermute | solution.py:26
  310.8 13.7 %collective-permute-start.21 = (bf16[24,3072]{1,0:T(8,128)(2,1)S(1)}, bf16[24,3072]{1,0:T(8,128)(2,1)S(1)}, u32[]{:S(2)}, u32[]{:S(2)}) collective-permute-start(bf16[24,3072]{1,0:T(8,128)(2,1)S(1)} %copy-done.18), channel_id=1, source_target_pairs={{0,16},{1,17},{2,18},{3,19},{4,20},{5,21},{6,22},{7,23},{8,24},{9,... | collective-permute-start | bytes 442376 | tf_op jit(solution)/shard_map/ppermute | solution.py:26
  312.9 11.6 %collective-permute-start.22 = (bf16[24,3072]{1,0:T(8,128)(2,1)S(1)}, bf16[24,3072]{1,0:T(8,128)(2,1)S(1)}, u32[]{:S(2)}, u32[]{:S(2)}) collective-permute-start(bf16[24,3072]{1,0:T(8,128)(2,1)S(1)} %copy-done.17), channel_id=1, source_target_pairs={{0,24},{1,25},{2,26},{3,27},{4,28},{5,29},{6,30},{7,31},{8,16},{9,... | collective-permute-start | bytes 442376 | tf_op jit(solution)/shard_map/ppermute | solution.py:26
  320.0 15.3 %collective-permute-start.18 = (bf16[24,3072]{1,0:T(8,128)(2,1)}, bf16[24,3072]{1,0:T(8,128)(2,1)S(1)}, u32[]{:S(2)}, u32[]{:S(2)}) collective-permute-start(bf16[24,3072]{1,0:T(8,128)(2,1)} %get-tuple-element.128), channel_id=1, source_target_pairs={{0,16},{1,17},{2,18},{3,19},{4,20},{5,21},{6,22},{7,23},{8,24},{9,... | collective-permute-start | bytes 442376 | tf_op jit(solution)/shard_map/ppermute | solution.py:26
  321.8 13.5 %collective-permute-start.19 = (bf16[24,3072]{1,0:T(8,128)(2,1)}, bf16[24,3072]{1,0:T(8,128)(2,1)S(1)}, u32[]{:S(2)}, u32[]{:S(2)}) collective-permute-start(bf16[24,3072]{1,0:T(8,128)(2,1)} %get-tuple-element.129), channel_id=1, source_target_pairs={{0,24},{1,25},{2,26},{3,27},{4,28},{5,29},{6,30},{7,31},{8,16},{9,... | collective-permute-start | bytes 442376 | tf_op jit(solution)/shard_map/ppermute | solution.py:26
  (41 other events, 267.7 us)
Sparse Core Ops, SparseCore 0:
  12.1 122.4 all-gather.1
